TPU v7x, 32 devices: a whole 2x2x4 slice. The times are simulated.
32 devices in a mesh: dp: 4 (over z), expert: 8 (over y, x, core).
Axes of the slice: x: 2, y: 2, z: 4, core: 2. Of those that a mesh axis runs over, the one named last changes fastest.
Arguments:
- tokens: bfloat16 [4096, 2048], P(('dp', 'expert')), may hold values from -6 to 6
- expert_ids: int32 [4096, 4], P(('dp', 'expert')), may hold values from 0 to 7, all different within a row; in each aligned block of 128 rows (0 to 127, 128 to 255, ...) at most 128 rows name the same one
- gates: bfloat16 [4096, 4], P(('dp', 'expert')), may hold values from 0.099609375 to 1
- w_gate: bfloat16 [8, 2048, 384], P('expert'), may hold values from -0.125 to 0.125
- w_up: bfloat16 [8, 2048, 384], P('expert'), may hold values from -0.125 to 0.125
- w_down: bfloat16 [8, 384, 2048], P('expert'), may hold values from -0.3125 to 0.3125
- cotangent: bfloat16 [4096, 2048], P(('dp', 'expert')), may hold values from -6 to 6
Outputs:
- mixed: bfloat16 [4096, 2048], P(('dp', 'expert'))
- grad_tokens: bfloat16 [4096, 2048], P(('dp', 'expert'))
- grad_gate: float32 [8, 2048, 384], P('expert', 'dp')
- grad_up: float32 [8, 2048, 384], P('expert', 'dp')
- grad_down: float32 [8, 384, 2048], P('expert', 'dp')
Inputs may be any that keep to these rules, and one draw needn't show every extreme that they name: `expert_ids`: each row names 4 different experts. In each aligned block of 128 rows (the rows of one device) no expert is named by more than 128 rows, a bound that some block reaches.
All inputs are finite; a program needn't handle non-finite values.
Results may differ from a plain program's by a relative error of at most 0.024.
Values may be sent and summed in bfloat16 or wider, within the bound.
No kernel may reach another device: no remote copies, remote signals or barrier semaphores. Data moves between devices by JAX's collectives and lax.ppermute only.
A program may use at most 128 MiB of HBM per device.

v0:
```python
import jax
import jax.numpy as jnp
from jax import lax
from jax.sharding import PartitionSpec as P


def expert_rows(inputs, out_grads, gate_col, gate_panel, up_panel, down_panel):
    pre_gate = jnp.dot(inputs, gate_panel, preferred_element_type=jnp.float32)
    pre_up = jnp.dot(inputs, up_panel, preferred_element_type=jnp.float32)
    gate_sigmoid = jax.nn.sigmoid(pre_gate)
    activated = (pre_gate * gate_sigmoid * pre_up).astype(jnp.bfloat16)
    expert_out = jnp.dot(activated, down_panel, preferred_element_type=jnp.float32)
    contrib = (gate_col.astype(jnp.float32)[:, None] * expert_out).astype(jnp.bfloat16)
    act_grad = lax.dot_general(
        out_grads, down_panel, (((1,), (1,)), ((), ())), preferred_element_type=jnp.float32
    )
    up_grad = (act_grad * pre_gate * gate_sigmoid).astype(jnp.bfloat16)
    pre_grad = (act_grad * pre_up * gate_sigmoid * (1.0 + pre_gate * (1.0 - gate_sigmoid))).astype(
        jnp.bfloat16
    )
    grad_rows = lax.dot_general(
        pre_grad, gate_panel, (((1,), (1,)), ((), ())), preferred_element_type=jnp.float32
    )
    grad_rows = grad_rows + lax.dot_general(
        up_grad, up_panel, (((1,), (1,)), ((), ())), preferred_element_type=jnp.float32
    )
    grad_rows = grad_rows.astype(jnp.bfloat16)
    wgrad_gate = lax.dot_general(
        inputs, pre_grad, (((0,), (0,)), ((), ())), preferred_element_type=jnp.float32
    )
    wgrad_up = lax.dot_general(
        inputs, up_grad, (((0,), (0,)), ((), ())), preferred_element_type=jnp.float32
    )
    wgrad_down = lax.dot_general(
        activated, out_grads, (((0,), (0,)), ((), ())), preferred_element_type=jnp.float32
    )
    return (contrib, grad_rows, wgrad_gate, wgrad_up, wgrad_down)


def slot_table(route_ids, expert_num, per_source):
    token_count, pick_count = route_ids.shape
    matches = route_ids == expert_num
    hit_rows = jnp.any(matches, axis=1).astype(jnp.int32)
    which_pick = jnp.sum(
        matches.astype(jnp.int32) * jnp.arange(pick_count, dtype=jnp.int32)[None, :], axis=1
    )
    rank_of = jnp.cumsum(hit_rows) - hit_rows
    wanted = jnp.arange(per_source, dtype=jnp.int32)
    chosen = ((hit_rows[None, :] == 1) & (rank_of[None, :] == wanted[:, None])).astype(jnp.int32)
    valid_slot = jnp.sum(chosen, axis=1) > 0
    row_of = jnp.sum(chosen * jnp.arange(token_count, dtype=jnp.int32)[None, :], axis=1)
    pick_of = jnp.sum(chosen * which_pick[None, :], axis=1)
    return (row_of, pick_of, valid_slot)


def per_device(tokens, expert_ids, gates, w_gate, w_up, w_down, cotangent):
    tok_dev, model_width = tokens.shape
    group_size = lax.axis_size("expert")
    slot_count = group_size * tok_dev
    my_expert = lax.axis_index("expert")
    gate_panel = w_gate[0]
    up_panel = w_up[0]
    down_panel = w_down[0]
    all_rows, all_cot, all_gates = (
        lax.all_gather(tokens, "expert", axis=0, tiled=True),
        lax.all_gather(cotangent, "expert", axis=0, tiled=True),
        lax.all_gather(gates, "expert", axis=0, tiled=True),
    )
    all_ids = lax.all_gather(expert_ids, "expert", axis=0, tiled=True)
    source_ids = all_ids.reshape(group_size, tok_dev, all_ids.shape[1])
    row_of, pick_of, keep_mask = jax.vmap(
        lambda route_ids: slot_table(route_ids, my_expert, tok_dev)
    )(source_ids)
    flat_row = (row_of + jnp.arange(group_size, dtype=jnp.int32)[:, None] * tok_dev).reshape(
        slot_count
    )
    keep_b = keep_mask.reshape(slot_count).astype(jnp.bfloat16)
    inputs = all_rows[flat_row] * keep_b[:, None]
    gate_col = all_gates[flat_row, pick_of.reshape(slot_count)] * keep_b
    out_grads = (
        gate_col.astype(jnp.float32)[:, None] * all_cot[flat_row].astype(jnp.float32)
    ).astype(jnp.bfloat16)
    contrib, grad_rows, acc_gate, acc_up, acc_down = expert_rows(
        inputs, out_grads, gate_col, gate_panel, up_panel, down_panel
    )
    dest = jnp.where(keep_mask.reshape(slot_count), flat_row, group_size * tok_dev)
    part_out = (
        jnp.zeros((group_size * tok_dev, model_width), jnp.float32)
        .at[dest]
        .set(contrib.astype(jnp.float32), mode="drop")
    )
    part_grad = (
        jnp.zeros((group_size * tok_dev, model_width), jnp.float32)
        .at[dest]
        .set(grad_rows.astype(jnp.float32), mode="drop")
    )
    summed_out, summed_grad = (
        lax.psum_scatter(
            part_out.astype(jnp.bfloat16), "expert", scatter_dimension=0, tiled=True
        ).astype(jnp.float32),
        lax.psum_scatter(
            part_grad.astype(jnp.bfloat16), "expert", scatter_dimension=0, tiled=True
        ).astype(jnp.float32),
    )
    mixed = summed_out.astype(jnp.bfloat16)
    grad_tokens = summed_grad.astype(jnp.bfloat16)
    grad_gate, grad_up, grad_down = (
        lax.psum_scatter(
            acc_gate.astype(jnp.bfloat16), "dp", scatter_dimension=0, tiled=True
        ).astype(jnp.float32),
        lax.psum_scatter(acc_up.astype(jnp.bfloat16), "dp", scatter_dimension=0, tiled=True).astype(
            jnp.float32
        ),
        lax.psum_scatter(
            acc_down.astype(jnp.bfloat16), "dp", scatter_dimension=0, tiled=True
        ).astype(jnp.float32),
    )
    return (mixed, grad_tokens, grad_gate[None], grad_up[None], grad_down[None])


def solution(mesh):
    return jax.shard_map(
        per_device,
        mesh=mesh,
        in_specs=(
            P(("dp", "expert"), None),
            P(("dp", "expert"), None),
            P(("dp", "expert"), None),
            P("expert", None, None),
            P("expert", None, None),
            P("expert", None, None),
            P(("dp", "expert"), None),
        ),
        out_specs=(
            P(("dp", "expert"), None),
            P(("dp", "expert"), None),
            P("expert", "dp", None),
            P("expert", "dp", None),
            P("expert", "dp", None),
        ),
        check_vma=False,
    )
```

profile of v0, /device:TPU:10, one launch (start us, length us, event | category | flops | bytes accessed | tf_op | source)
XLA Modules:
  0.0 334.9 jit_solution(15715680986496251538)
XLA Ops:
  7.2 0.7 all-gather.3.cloned.1.call-update
  8.0 0.7 all-gather.5.cloned.1.call-update
  8.7 8.9 %all_gather.12 = s32[1024,4]{0,1:T(4,128)S(1)} all-gather(s32[128,4]{0,1:T(4,128)} %param.8), channel_id=1, replica_groups=mesh['dp'=4,'expert'=8] {'expert'}, dimensions={0}, use_global_device_ids=true | all-gather | bytes 18432 | tf_op jit(solution)/shard_map/all_gather | solution.py:69
  17.7 0.3 reduce_window_sum.11
  17.9 8.1 %all_gather.13 = bf16[1024,4]{0,1:T(4,128)(2,1)S(1)} all-gather(bf16[128,4]{0,1:T(4,128)(2,1)} %param.9), channel_id=1, replica_groups=mesh['dp'=4,'expert'=8] {'expert'}, dimensions={0}, use_global_device_ids=true | all-gather | bytes 9216 | tf_op jit(solution)/shard_map/all_gather | solution.py:67
  26.0 0.5 select_reduce_fusion
  26.6 9.1 %gather_fusion = bf16[1024]{0:T(1024)(128)(2,1)S(1)} fusion(bf16[1024,4]{0,1:T(4,128)(2,1)S(1)} %all_gather.13, s32[1024]{0:T(1024)S(1)} %bitcast.58), kind=kCustom, calls=%fused_computation | custom fusion | bytes 12288 | tf_op jit(solution)/shard_map/gather | solution.py:79
  35.7 12.1 %all-gather.3.cloned.1.call-done = bf16[1024,2048]{1,0:T(8,128)(2,1)} async-done(((bf16[128,2048]{1,0:T(8,128)(2,1)}), bf16[1024,2048]{1,0:T(8,128)(2,1)}) %all-gather.3.cloned.1.call-update) | async-done | bytes 4194320 | tf_op jit(solution)/shard_map/all_gather | solution.py:65
  47.8 11.6 %gather_fusion.1 = bf16[1024,2048]{1,0:T(8,128)(2,1)} fusion(bf16[1024,2048]{1,0:T(8,128)(2,1)} %all-gather.3.cloned.1.call-done, s32[1024]{0:T(1024)S(1)} %broadcast_clamp_fusion), kind=kCustom, calls=%fused_computation.1 | custom fusion | bytes 8392704 | tf_op jit(solution)/shard_map/gather | solution.py:78
  59.4 6.3 %fusion.8 = f32[1024,384]{1,0:T(8,128)} fusion(bf16[1024,2048]{1,0:T(8,128)(2,1)} %gather_fusion.1, bf16[1024]{0:T(1024)(128)(2,1)S(1)} %bitcast_convert_fusion.3, bf16[1,2048,384]{2,1,0:T(8,128)(2,1)} %param.11), kind=kOutput, calls=%fused_computation.19 | convolution fusion | flops 1612709888 | bytes 7342080 | tf_op jit(solution)/shard_map/dot_general | solution.py:9
  65.7 3.6 %fusion.10 = f32[1024,384]{1,0:T(8,128)} fusion(bf16[1024,2048]{1,0:T(8,128)(2,1)S(1)} %copy-done.1, bf16[1024]{0:T(1024)(128)(2,1)S(1)} %bitcast_convert_fusion.3, bf16[1,2048,384]{2,1,0:T(8,128)(2,1)S(1)} %copy-done.3), kind=kOutput, calls=%fused_computation.21 | convolution fusion | flops 1612709888 | bytes 7342080 | tf_op jit(solution)/shard_map/dot_general | solution.py:8
  69.3 17.2 %all-gather.5.cloned.1.call-done = bf16[1024,2048]{1,0:T(8,128)(2,1)} async-done(((bf16[128,2048]{1,0:T(8,128)(2,1)}), bf16[1024,2048]{1,0:T(8,128)(2,1)}) %all-gather.5.cloned.1.call-update) | async-done | bytes 4194320 | tf_op jit(solution)/shard_map/all_gather | solution.py:66
  86.5 11.6 %gather_fusion.2 = bf16[1024,2048]{1,0:T(8,128)(2,1)} fusion(bf16[1024,2048]{1,0:T(8,128)(2,1)} %all-gather.5.cloned.1.call-done, s32[1024]{0:T(1024)S(1)} %broadcast_clamp_fusion), kind=kCustom, calls=%fused_computation.2 | custom fusion | bytes 8392704 | tf_op jit(solution)/shard_map/gather | solution.py:81
  98.0 7.3 %multiply_convert_fusion.4 = (bf16[1024,384]{1,0:T(8,128)(2,1)S(1)}, bf16[1024,384]{1,0:T(8,128)(2,1)}, bf16[1024,384]{1,0:T(8,128)(2,1)}) fusion(f32[1024,384]{1,0:T(8,128)} %fusion.10, f32[1024,384]{1,0:T(8,128)} %fusion.8, bf16[1,384,2048]{2,1,0:T(8,128)(2,1)S(1)} %copy-done, bf16[1024,2048]{1,0:T(8,128)(2,1)} %gather_fusion.2, ...), kind=kOutput, calls=%fused_computation.35 | convolution fusion | flops 1623195648 | bytes 11276288 | tf_op jit(solution)/shard_map/dot_general | solution.py:14
  105.4 0.9 copy-done.5
  106.2 3.7 %convolution_convert_fusion.1 = bf16[2048,384]{1,0:T(8,128)(2,1)} fusion(bf16[1024,384]{1,0:T(8,128)(2,1)S(1)} %get-tuple-element.12, bf16[1024,2048]{1,0:T(8,128)(2,1)S(1)} %copy-done.2, bf16[1024]{0:T(1024)(128)(2,1)S(1)} %bitcast_convert_fusion.3), kind=kOutput, calls=%fused_computation.15 | convolution fusion | flops 1613496320 | bytes 6555648 | tf_op jit(solution)/shard_map/dot_general | solution.py:31
  110.2 6.0 %convolution_convert_fusion.2 = bf16[2048,384]{1,0:T(8,128)(2,1)} fusion(bf16[1024,384]{1,0:T(8,128)(2,1)} %get-tuple-element.13, bf16[1024,2048]{1,0:T(8,128)(2,1)} %gather_fusion.1, bf16[1024]{0:T(1024)(128)(2,1)S(1)} %bitcast_convert_fusion.3), kind=kOutput, calls=%fused_computation.16 | convolution fusion | flops 1613496320 | bytes 6555648 | tf_op jit(solution)/shard_map/dot_general | solution.py:28
  116.3 5.6 %convolution_convert_fusion = bf16[384,2048]{1,0:T(8,128)(2,1)} fusion(bf16[1024,384]{1,0:T(8,128)(2,1)} %get-tuple-element.14, bf16[1024,2048]{1,0:T(8,128)(2,1)} %gather_fusion.2, f32[1024]{0:T(1024)S(1)} %get-tuple-element.8), kind=kOutput, calls=%fused_computation.14 | convolution fusion | flops 1617690624 | bytes 6557696 | tf_op jit(solution)/shard_map/dot_general | solution.py:34
  122.0 5.4 %multiply_convert_fusion.1 = bf16[1024,2048]{1,0:T(8,128)(2,1)} fusion(bf16[1024,384]{1,0:T(8,128)(2,1)} %get-tuple-element.14, f32[1024]{0:T(1024)S(1)} %get-tuple-element.8, bf16[1,384,2048]{2,1,0:T(8,128)(2,1)S(1)} %copy-done), kind=kOutput, calls=%fused_computation.11 | convolution fusion | flops 1614807040 | bytes 6557696 | tf_op jit(solution)/shard_map/dot_general | solution.py:12
  127.5 10.9 %scatter_custom_fusion = f32[1024,2048]{1,0:T(8,128)} fusion(s32[1024]{0:T(1024)S(1)} %bitcast.65, bf16[1024,2048]{1,0:T(8,128)(2,1)} %multiply_convert_fusion.1, f32[]{:T(128)} %constant.10.clone.1), kind=kCustom, calls=%fused_computation.9 | custom fusion | flops 2097152 | bytes 12582916 | tf_op jit(solution)/shard_map/scatter | solution.py:90
  138.4 6.1 %convert_element_type.93 = bf16[1024,2048]{1,0:T(8,128)(2,1)} convert(f32[1024,2048]{1,0:T(8,128)} %scatter_custom_fusion) | non-fusion elementwise | flops 2097152 | bytes 12582912 | tf_op jit(solution)/shard_map/convert_element_type | solution.py:99
  144.8 3.6 %fusion.21 = f32[1024,2048]{1,0:T(8,128)S(1)} fusion(bf16[1024,384]{1,0:T(8,128)(2,1)} %get-tuple-element.13, bf16[1,2048,384]{2,1,0:T(8,128)(2,1)S(1)} %copy-done.3), kind=kOutput, calls=%fused_computation.32 | convolution fusion | flops 1610612736 | bytes 10747904 | tf_op jit(solution)/shard_map/dot_general | solution.py:21
  148.4 4.3 %add_convert_fusion = bf16[1024,2048]{1,0:T(8,128)(2,1)} fusion(f32[1024,2048]{1,0:T(8,128)S(1)} %fusion.21, bf16[1024,384]{1,0:T(8,128)(2,1)S(1)} %copy-done.6, bf16[1,2048,384]{2,1,0:T(8,128)(2,1)S(1)} %copy-done.4), kind=kOutput, calls=%fused_computation.7 | convolution fusion | flops 1614807040 | bytes 14942208 | tf_op jit(solution)/shard_map/dot_general | solution.py:24
  152.8 10.9 %scatter_custom_fusion.1 = f32[1024,2048]{1,0:T(8,128)} fusion(s32[1024]{0:T(1024)S(1)} %bitcast.66, bf16[1024,2048]{1,0:T(8,128)(2,1)} %add_convert_fusion, f32[]{:T(128)} %constant.10.clone.1), kind=kCustom, calls=%fused_computation.5 | custom fusion | flops 2097152 | bytes 12582916 | tf_op jit(solution)/shard_map/scatter | solution.py:95
  163.7 6.1 %convert_element_type.100 = bf16[1024,2048]{1,0:T(8,128)(2,1)} convert(f32[1024,2048]{1,0:T(8,128)} %scatter_custom_fusion.1) | non-fusion elementwise | flops 2097152 | bytes 12582912 | tf_op jit(solution)/shard_map/convert_element_type | solution.py:102
  169.8 1.9 bitcast_convert_fusion.1
  171.8 9.0 %reduce-scatter.10.cloned.1.call-done = bf16[512,384]{1,0:T(8,128)(2,1)} async-done(((bf16[2048,384]{1,0:T(8,128)(2,1)}), bf16[512,384]{1,0:T(8,128)(2,1)}) %reduce-scatter.10.cloned.1.call-update) | async-done | bytes 393232 | tf_op jit(solution)/shard_map/reduce_scatter | solution.py:108
  180.8 1.9 bitcast_convert_fusion.2
  182.7 34.5 %reduce-scatter.14.cloned.1.call-done = bf16[96,2048]{1,0:T(8,128)(2,1)} async-done(((bf16[384,2048]{1,0:T(8,128)(2,1)}), bf16[96,2048]{1,0:T(8,128)(2,1)}) %reduce-scatter.14.cloned.1.call-update) | async-done | bytes 393232 | tf_op jit(solution)/shard_map/reduce_scatter | solution.py:114
  217.2 1.9 bitcast_convert_fusion
  219.2 53.2 %reduce-scatter.6.cloned.1.call-done = bf16[128,2048]{1,0:T(8,128)(2,1)} async-done(((bf16[1024,2048]{1,0:T(8,128)(2,1)}), bf16[128,2048]{1,0:T(8,128)(2,1)}) %reduce-scatter.6.cloned.1.call-update) | async-done | bytes 524304 | tf_op jit(solution)/shard_map/reduce_scatter | solution.py:98
  272.4 55.6 %reduce-scatter.8.cloned.1.call-done = bf16[128,2048]{1,0:T(8,128)(2,1)} async-done(((bf16[1024,2048]{1,0:T(8,128)(2,1)}), bf16[128,2048]{1,0:T(8,128)(2,1)}) %reduce-scatter.8.cloned.1.call-update) | async-done | bytes 524304 | tf_op jit(solution)/shard_map/reduce_scatter | solution.py:101
  (38 shorter events, 1.0 us)
Async XLA Ops:
  7.2 90.9 %copy-start = (bf16[1,384,2048]{2,1,0:T(8,128)(2,1)S(1)}, bf16[1,384,2048]{2,1,0:T(8,128)(2,1)}, u32[]{:S(2)}) copy-start(bf16[1,384,2048]{2,1,0:T(8,128)(2,1)} %param.12) | copy-start | bytes 4718596
  7.2 40.7 %all-gather.3.cloned.1.call-start = ((), (), s32[]{:S(2)}) async-start(), calls=%async_computation.5 | async-start | bytes 4718592 | tf_op jit(solution)/shard_map/all_gather | solution.py:65
  7.9 78.6 %all-gather.5.cloned.1.call-start = ((), (), s32[]{:S(2)}) async-start(), calls=%async_computation.7 | async-start | bytes 4718592 | tf_op jit(solution)/shard_map/all_gather | solution.py:66
  8.7 161.2 %reduce-scatter.12.cloned.1.call-start = ((), (), s32[]{:S(2)}) async-start(), calls=%async_computation.10 | async-start | bytes 1966080 | tf_op jit(solution)/shard_map/reduce_scatter | solution.py:111
  59.4 6.3 %copy-start.1 = (bf16[1024,2048]{1,0:T(8,128)(2,1)S(1)}, bf16[1024,2048]{1,0:T(8,128)(2,1)}, u32[]{:S(2)}) copy-start(bf16[1024,2048]{1,0:T(8,128)(2,1)} %gather_fusion.1) | copy-start | bytes 12582916
  59.4 6.3 %copy-start.3 = (bf16[1,2048,384]{2,1,0:T(8,128)(2,1)S(1)}, bf16[1,2048,384]{2,1,0:T(8,128)(2,1)}, u32[]{:S(2)}) copy-start(bf16[1,2048,384]{2,1,0:T(8,128)(2,1)} %param.10) | copy-start | bytes 4718596
  98.0 8.2 %copy-start.2 = (bf16[1024,2048]{1,0:T(8,128)(2,1)S(1)}, bf16[1024,2048]{1,0:T(8,128)(2,1)}, u32[]{:S(2)}) copy-start(bf16[1024,2048]{1,0:T(8,128)(2,1)} %gather_fusion.1) | copy-start | bytes 12582916
  105.4 0.9 copy-start.5
  110.0 70.8 %reduce-scatter.10.cloned.1.call-start = ((), (), s32[]{:S(2)}) async-start(), calls=%async_computation.9 | async-start | bytes 1966080 | tf_op jit(solution)/shard_map/reduce_scatter | solution.py:108
  116.3 100.9 %reduce-scatter.14.cloned.1.call-start = ((), (), s32[]{:S(2)}) async-start(), calls=%async_computation.11 | async-start | bytes 1966080 | tf_op jit(solution)/shard_map/reduce_scatter | solution.py:114
  121.9 150.4 %reduce-scatter.6.cloned.1.call-start = ((), (), s32[]{:S(2)}) async-start(), calls=%async_computation.6 | async-start | bytes 4718592 | tf_op jit(solution)/shard_map/reduce_scatter | solution.py:98
  144.5 183.5 %reduce-scatter.8.cloned.1.call-start = ((), (), s32[]{:S(2)}) async-start(), calls=%async_computation.8 | async-start | bytes 4718592 | tf_op jit(solution)/shard_map/reduce_scatter | solution.py:101
  144.7 3.7 %copy-start.4 = (bf16[1,2048,384]{2,1,0:T(8,128)(2,1)S(1)}, bf16[1,2048,384]{2,1,0:T(8,128)(2,1)}, u32[]{:S(2)}) copy-start(bf16[1,2048,384]{2,1,0:T(8,128)(2,1)} %param.11) | copy-start | bytes 4718596
  144.8 3.7 %copy-start.6 = (bf16[1024,384]{1,0:T(8,128)(2,1)S(1)}, bf16[1024,384]{1,0:T(8,128)(2,1)}, u32[]{:S(2)}) copy-start(bf16[1024,384]{1,0:T(8,128)(2,1)} %copy-done.5) | copy-start | bytes 2359300
Sparse Core Ops, SparseCore 0:
  9.9 37.8 all-gather.2
  49.7 36.7 all-gather.4
  110.1 34.1 reduce-scatter.11
  146.5 34.2 reduce-scatter.9
  182.9 34.2 reduce-scatter.13
  221.0 51.3 reduce-scatter.5
  276.7 51.2 reduce-scatter.7
where the time goes:
time: 337 us; the launch traced here: 335 us
  waiting for transfers between devices  183 us (54%)
  matrix products  46 us (14%)
  other arithmetic  40.7 us (12%)
  local copies, waits for them, and re-layouts  33.1 us (10%)
  blocking collectives  17 us (5%)
  between operations  14.3 us (4%)
    reduce_scatter x1, waiting for transfers between devices, per_device(): lax.psum_scatter(part_grad.astype(jnp.bfloat16), 'expert', scatter_dimens...  55.6 us
    reduce_scatter x1, waiting for transfers between devices, per_device(): lax.psum_scatter(part_out.astype(jnp.bfloat16), 'expert', scatter_dimensi...  53.2 us
    reduce_scatter x1, waiting for transfers between devices, per_device(): lax.psum_scatter(acc_down.astype(jnp.bfloat16), 'dp', scatter_dimension=0...  34.5 us
    all_gather x1, waiting for transfers between devices, per_device(): lax.all_gather(cotangent, 'expert', axis=0, tiled=True)  17.2 us
    all_gather x1, waiting for transfers between devices, per_device(): lax.all_gather(tokens, 'expert', axis=0, tiled=True)  12.1 us
    gather x1, local copies, waits for them, and re-layouts, per_device(): inputs = all_rows[flat_row] * keep_b[:, None]  11.6 us
    gather x1, local copies, waits for them, and re-layouts, per_device(): all_cot[flat_row].astype(jnp.float32)  11.6 us
    scatter x1, other arithmetic, per_device(): part_grad = jnp.zeros((group_size * tok_dev, model_width), jnp.float32).a...  10.9 us
  transfers between devices with their start and end apart: 7, of which 6 were waited for; matrix products, arithmetic and copies ran while one was open for 29% of the time, Pallas kernels for 0%

commit v1 on v0

v1 whole, which is shorter than its diff:
```python
import functools

import jax
import jax.numpy as jnp
from jax import lax
from jax.experimental import pallas as pl
from jax.experimental.pallas import tpu as pltpu
from jax.sharding import PartitionSpec as P

F32 = jnp.float32
BF16 = jnp.bfloat16
LANES = 128
CORE, NEAR, FAR = 1, 2, 4
PARAMS = pltpu.CompilerParams(vmem_limit_bytes=60 * 1024 * 1024)
ANY = pl.BlockSpec(memory_space=pl.ANY)
SMEM = pl.BlockSpec(memory_space=pltpu.SMEM)
NT = (((1,), (1,)), ((), ()))


def cost(flops, arrays):
    size = sum(a.size * a.dtype.itemsize for a in arrays)
    return pl.CostEstimate(flops=flops // 64, bytes_accessed=size // 64, transcendentals=0)


def own_gate(gate_rows, expert_num):
    lane = lax.broadcasted_iota(jnp.int32, gate_rows.shape, 1)
    kept = jnp.where(lane == expert_num, gate_rows.astype(F32), 0.0)
    return jnp.sum(kept, axis=1, keepdims=True)


def hidden_kernel(blocks, *refs):
    me_ref = refs[0]
    toks, cots = refs[1 : 1 + blocks], refs[1 + blocks : 1 + 2 * blocks]
    wg_hbm, wu_hbm, wd_hbm = refs[1 + 2 * blocks : 4 + 2 * blocks]
    act_ref, hid_ref, act_t_ref, hid_t_ref, og_hbm = refs[4 + 2 * blocks : 9 + 2 * blocks]
    rows, gates, cot, wide, down, og, sems = refs[9 + 2 * blocks :]
    each, width = cots[0].shape
    hid = wg_hbm.shape[1]

    def copy(source, target, number):
        made = pltpu.make_async_copy(source, target, sems.at[number])
        made.start()
        return made

    first = [copy(wg_hbm, wide.at[:, :hid], 0), copy(wu_hbm, wide.at[:, hid:], 1)]
    for i in range(blocks):
        at = pl.ds(i * each, each)
        first.append(copy(toks[i].at[:, :width], rows.at[at, :], 3 + 3 * i))
    second = []
    for i in range(blocks):
        at = pl.ds(i * each, each)
        second.append(copy(toks[i].at[:, width:], gates.at[at, :], 4 + 3 * i))
        second.append(copy(cots[i], cot.at[at, :], 5 + 3 * i))
    second.append(copy(wd_hbm, down, 2))
    for made in first:
        made.wait()
    pre = jnp.dot(rows[...], wide[...], preferred_element_type=F32)
    for made in second:
        made.wait()
    og[...] = (own_gate(gates[...], me_ref[0]) * cot[...].astype(F32)).astype(BF16)
    out = pltpu.make_async_copy(og, og_hbm, sems.at[0])
    out.start()
    act_grad = lax.dot_general(og[...], down[...], NT, preferred_element_type=F32)
    pre_gate, pre_up = pre[:, :hid], pre[:, hid:]
    s = 1.0 / (1.0 + jnp.exp(-pre_gate))
    act = (pre_gate * s * pre_up).astype(BF16)
    pre_grad = (act_grad * pre_up * s * (1.0 + pre_gate * (1.0 - s))).astype(BF16)
    up_grad = (act_grad * pre_gate * s).astype(BF16)
    act_ref[...] = act
    act_t_ref[...] = act.T
    hid_ref[:, :hid] = pre_grad
    hid_ref[:, hid:] = up_grad
    hid_t_ref[:hid, :] = pre_grad.T
    hid_t_ref[hid:, :] = up_grad.T
    out.wait()


def hidden(me, toks, cots, wg, wu, wd):
    blocks = len(toks)
    each = cots[0].shape[0]
    rows = blocks * each
    width, hid = wg.shape
    shapes = [(rows, hid), (rows, 2 * hid), (hid, rows), (2 * hid, rows)]
    outs = tuple(jax.ShapeDtypeStruct(s, BF16) for s in shapes + [(rows, width)])
    specs = tuple(pl.BlockSpec(s, lambda i: (0, 0)) for s in shapes) + (ANY,)
    return pl.pallas_call(
        functools.partial(hidden_kernel, blocks),
        out_shape=outs,
        grid=(1,),
        in_specs=[SMEM] + [ANY] * (2 * blocks + 3),
        out_specs=specs,
        scratch_shapes=[
            pltpu.VMEM((rows, width), BF16),
            pltpu.VMEM((rows, LANES), BF16),
            pltpu.VMEM((rows, width), BF16),
            pltpu.VMEM((width, 2 * hid), BF16),
            pltpu.VMEM((hid, width), BF16),
            pltpu.VMEM((rows, width), BF16),
            pltpu.SemaphoreType.DMA((3 + 3 * blocks,)),
        ],
        compiler_params=PARAMS,
        cost_estimate=cost(6 * rows * width * hid, (*toks, *cots, wg, wu, wd) + outs),
    )(me, *toks, *cots, wg, wu, wd)


def rows_kernel(blocks, more, *refs):
    me_ref, gates, refs = refs[0], refs[1 : 1 + blocks], refs[1 + blocks :]
    act_ref, hid_ref, wg_hbm, wu_hbm, wd_hbm = refs[:5]
    added = refs[5 : 5 + more]
    outs, (wide, down, sems) = refs[5 + more : -3], refs[-3:]
    hid = wg_hbm.shape[1]
    copies = [
        pltpu.make_async_copy(wd_hbm, down, sems.at[0]),
        pltpu.make_async_copy(wg_hbm, wide.at[:, :hid], sems.at[1]),
        pltpu.make_async_copy(wu_hbm, wide.at[:, hid:], sems.at[2]),
    ]
    for made in copies:
        made.start()
    gate_col = own_gate(jnp.concatenate([g[...] for g in gates], axis=0), me_ref[0])
    half = len(outs) // 2

    def put(values, number):
        if more:
            values = values.astype(F32) + added[number][...].astype(F32)
        values = values.astype(BF16)
        each = values.shape[0] // half
        for i in range(half):
            outs[number * half + i][...] = values[i * each : (i + 1) * each]

    copies[0].wait()
    expert_out = jnp.dot(act_ref[...], down[...], preferred_element_type=F32)
    put((gate_col * expert_out).astype(BF16), 0)
    copies[1].wait()
    copies[2].wait()
    grad = lax.dot_general(hid_ref[...], wide[...], NT, preferred_element_type=F32)
    put(grad.astype(BF16), 1)


def rows_out(me, gate_arrays, act, hid, part, parts, wg, wu, wd, added, split):
    blocks = len(gate_arrays)
    each = gate_arrays[0].shape[0]
    rows = blocks * each
    assert rows * parts == act.shape[0]
    width, hidden_size = wg.shape
    out = jax.ShapeDtypeStruct((rows // split, width), BF16)
    gate_spec = pl.BlockSpec((each, LANES), lambda i: (0, width // LANES))
    return pl.pallas_call(
        functools.partial(rows_kernel, blocks, len(added)),
        out_shape=(out,) * (2 * split),
        grid=(1,),
        in_specs=[SMEM]
        + [gate_spec] * blocks
        + [pl.BlockSpec((rows, a.shape[1]), lambda i: (part, 0)) for a in (act, hid)]
        + [ANY] * 3
        + [pl.BlockSpec(a.shape, lambda i: (0, 0)) for a in added],
        out_specs=(pl.BlockSpec(out.shape, lambda i: (0, 0)),) * (2 * split),
        scratch_shapes=[
            pltpu.VMEM((width, 2 * hidden_size), BF16),
            pltpu.VMEM((hidden_size, width), BF16),
            pltpu.SemaphoreType.DMA((3,)),
        ],
        compiler_params=PARAMS,
        cost_estimate=cost(6 * rows * width * hidden_size, (wg, wu, wd) + tuple(added) + (out,) * (2 * split)),
    )(me, *gate_arrays, act, hid, wg, wu, wd, *added)


def wide_grad_kernel(groups, first, count, order_ref, *refs):
    blocks = sum(groups)
    toks, hids, outs = refs[:blocks], refs[blocks : blocks + len(groups)], refs[blocks + len(groups) :]
    total, at = None, 0
    for hid_ref, size in zip(hids, groups):
        rows = jnp.concatenate([t[...] for t in toks[at : at + size]], axis=0)
        part = jnp.dot(hid_ref[...], rows, preferred_element_type=F32)
        total = part if total is None else total + part
        at += size
    total = total.astype(BF16)
    for k in range(count):

        @pl.when(pl.program_id(0) == k)
        def _():
            outs[k][...] = total


def wide_grads(order, toks, hids, width, first, count):
    blocks = len(toks)
    each = toks[0].shape[0]
    groups = tuple(h.shape[1] // each for h in hids)
    both, tile = hids[0].shape[0], width // 4
    out = jax.ShapeDtypeStruct((both, tile), BF16)
    return pl.pallas_call(
        functools.partial(wide_grad_kernel, groups, first, count),
        out_shape=(out,) * count,
        grid_spec=pltpu.PrefetchScalarGridSpec(
            num_scalar_prefetch=1,
            grid=(count,),
            in_specs=[pl.BlockSpec((each, tile), lambda i, order: (0, order[first + i]))] * blocks
            + [pl.BlockSpec(h.shape, lambda i, order: (0, 0)) for h in hids],
            out_specs=(pl.BlockSpec(out.shape, lambda i, order: (0, 0)),) * count,
        ),
        compiler_params=PARAMS,
        cost_estimate=cost(2 * count * blocks * each * both * tile, tuple(hids) + (out,) * count),
    )(order, *toks, *hids)


def down_grad_kernel(groups, order_ref, *refs):
    acts, ogs, outs, full = refs[:groups], refs[groups : 2 * groups], refs[2 * groups : -1], refs[-1]
    total = None
    for act, og in zip(acts, ogs):
        part = jnp.dot(act[...], og[...], preferred_element_type=F32)
        total = part if total is None else total + part
    full[...] = total
    size = full.shape[0] // 4
    for k in range(4):
        at = pl.multiple_of(order_ref[k] * size, size)
        outs[k][...] = full[pl.ds(at, size), :].astype(BF16)


def down_grads(order, acts, ogs):
    hid = acts[0].shape[0]
    rows = sum(a.shape[1] for a in acts)
    width = ogs[0].shape[1]
    tile = width // 4
    out = jax.ShapeDtypeStruct((hid // 4, width), BF16)
    return pl.pallas_call(
        functools.partial(down_grad_kernel, len(acts)),
        out_shape=(out,) * 4,
        grid_spec=pltpu.PrefetchScalarGridSpec(
            num_scalar_prefetch=1,
            grid=(width // tile,),
            in_specs=[pl.BlockSpec(a.shape, lambda i, order: (0, 0)) for a in acts]
            + [pl.BlockSpec((o.shape[0], tile), lambda i, order: (0, i)) for o in ogs],
            out_specs=(pl.BlockSpec((hid // 4, tile), lambda i, order: (0, i)),) * 4,
            scratch_shapes=[pltpu.VMEM((hid, tile), F32)],
        ),
        compiler_params=PARAMS,
        cost_estimate=cost(2 * rows * hid * width, tuple(acts) + tuple(ogs)),
    )(order, *acts, *ogs)


def turn_kernel(mid_ref, own, a1, a2, a3, a4, gate_ref, up_ref):
    ends = a1[...].astype(F32) + a2[...].astype(F32)
    total = own[...].astype(F32) + (a3[...].astype(F32) + a4[...].astype(F32))
    total = (total + jnp.where(mid_ref[0] == 1, 0.0, ends)).T
    hid = gate_ref.shape[1]
    gate_ref[...] = total[:, :hid]
    up_ref[...] = total[:, hid:]


def turn(mid, terms):
    both, tile = terms[0].shape
    out = jax.ShapeDtypeStruct((tile, both // 2), F32)
    return pl.pallas_call(
        turn_kernel,
        out_shape=(out, out),
        grid=(tile // LANES,),
        in_specs=[SMEM] + [pl.BlockSpec((both, LANES), lambda i: (0, i))] * 5,
        out_specs=(pl.BlockSpec((LANES, both // 2), lambda i: (i, 0)),) * 2,
        compiler_params=PARAMS,
        cost_estimate=cost(5 * both * tile, terms + (out, out)),
    )(mid, *terms)


def after(values, earlier):
    return lax.optimization_barrier((values, earlier))[0]


def add(a, b):
    return (a.astype(F32) + b.astype(F32)).astype(BF16)


def line_terms(parts, mid):
    move = lambda a, pairs: lax.ppermute(a, "dp", pairs)
    one = move(parts[0], [(0, 1), (1, 0), (2, 3), (3, 2)])
    two = move(add(parts[1], jnp.where(mid, one, jnp.zeros_like(one))), [(0, 1), (1, 3), (3, 2), (2, 0)])
    three = move(parts[2], [(0, 1), (3, 2)])
    four = move(add(parts[2], two), [(1, 2), (2, 1)])
    return (parts[3], one, two, three, four)


LINE_ORDER = ((3, 2, 1, 0), (0, 3, 2, 1), (3, 0, 1, 2), (0, 1, 2, 3))


def per_device(tokens, expert_ids, gates, w_gate, w_up, w_down, cotangent):
    width = tokens.shape[1]
    group = lax.axis_size("expert")
    shards = lax.axis_size("dp")
    assert group == 8
    me = lax.axis_index("expert").astype(jnp.int32).reshape(1)
    z = lax.axis_index("dp")
    wg, wu, wd = w_gate[0], w_up[0], w_down[0]

    def flip(array, bit):
        return lax.ppermute(array, "expert", [(i, i ^ bit) for i in range(group)])

    cot_0 = cotangent
    cot_y = flip(cot_0, FAR)
    cot_x = flip(cot_0, NEAR)
    lanes = jnp.arange(LANES, dtype=jnp.int32)[None, None, :]
    spread = jnp.where(expert_ids[:, :, None] == lanes, gates.astype(F32)[:, :, None], 0.0)
    tok_0 = jnp.concatenate([tokens, jnp.sum(spread, axis=1).astype(BF16)], axis=1)
    tok_x = flip(tok_0, NEAR)
    tok_y = flip(tok_0, FAR)
    cot_d = flip(cot_y, NEAR)
    tok_d = flip(tok_x, FAR)

    toks_a, cots_a = [tok_0, tok_x, tok_y], [cot_0, cot_x, cot_y]
    toks_a += [flip(t, CORE) for t in toks_a]
    cots_a += [flip(c, CORE) for c in cots_a]
    toks_b, cots_b = [tok_d, flip(tok_d, CORE)], [cot_d, flip(cot_d, CORE)]
    act_a, hid_a, act_t_a, hid_t_a, og_a = hidden(me, toks_a, cots_a, wg, wu, wd)
    act_b, hid_b, act_t_b, hid_t_b, og_b = hidden(me, toks_b, cots_b, wg, wu, wd)

    line = shards == 4
    table = jnp.asarray(LINE_ORDER if line else ((0, 1, 2, 3),), jnp.int32)
    order = table[z if line else 0]
    toks = toks_a + toks_b
    wide = wide_grads(order, toks, (hid_t_a, hid_t_b), width, 0, 1)
    act_t_a, act_b = after((act_t_a, act_b), wide[0])
    down = down_grads(order, (act_t_a, act_t_b), (og_a, og_b))
    act_b, hid_t_a = after((act_b, hid_t_a), down[0])
    out_s, grad_s = rows_out(me, toks_b[1:], act_b, hid_b, 1, 2, wg, wu, wd, (), 1)
    hid_t_a = after(hid_t_a, out_s)
    wide = wide + wide_grads(order, toks, (hid_t_a, hid_t_b), width, 1, 3)
    added = after((flip(out_s, CORE), flip(grad_s, CORE)), wide[1])
    out_d, grad_d = rows_out(me, toks_b[:1], act_b, hid_b, 0, 2, wg, wu, wd, added, 1)
    act_a = after(act_a, out_d)
    hid_size = wg.shape[1]
    if line:
        mid = (z == 1) | (z == 2)
        wide_terms = line_terms(wide, mid)
        down_terms = line_terms(down, mid)
        grad_gate, grad_up = turn(mid.astype(jnp.int32).reshape(1), wide_terms)
        own, one, two, three, four = (t.astype(F32) for t in down_terms)
        grad_down = own + (three + four) + jnp.where(mid, 0.0, one + two)
    else:
        wide_all = jnp.concatenate(wide, axis=1).T
        grad_wide = lax.psum_scatter(wide_all, "dp", scatter_dimension=0, tiled=True).astype(F32)
        grad_gate, grad_up = grad_wide[:, :hid_size], grad_wide[:, hid_size:]
        grad_down = lax.psum_scatter(jnp.concatenate(down, axis=0), "dp", scatter_dimension=0, tiled=True).astype(F32)

    out_s, grad_s = rows_out(me, toks_a[3:], act_a, hid_a, 1, 2, wg, wu, wd, (), 1)
    out_0, out_x, out_y, grad_0, grad_x, grad_y = rows_out(
        me, toks_a[:3], act_a, hid_a, 0, 2, wg, wu, wd, (flip(out_s, CORE), flip(grad_s, CORE)), 3
    )
    out_y = add(out_y, flip(out_d, NEAR))
    grad_x = add(grad_x, flip(grad_d, FAR))
    mixed = out_0.astype(F32) + flip(out_x, NEAR).astype(F32) + flip(out_y, FAR).astype(F32)
    grad_tokens = grad_0.astype(F32) + flip(grad_y, FAR).astype(F32) + flip(grad_x, NEAR).astype(F32)
    return (mixed.astype(BF16), grad_tokens.astype(BF16), grad_gate[None], grad_up[None], grad_down[None])


def solution(mesh):
    return jax.shard_map(
        per_device,
        mesh=mesh,
        in_specs=(
            P(("dp", "expert"), None),
            P(("dp", "expert"), None),
            P(("dp", "expert"), None),
            P("expert", None, None),
            P("expert", None, None),
            P("expert", None, None),
            P(("dp", "expert"), None),
        ),
        out_specs=(
            P(("dp", "expert"), None),
            P(("dp", "expert"), None),
            P("expert", "dp", None),
            P("expert", "dp", None),
            P("expert", "dp", None),
        ),
        check_vma=False,
    )
```

time: 337 us -> 184 us (0.55)
  waiting for transfers between devices: 183 us -> 68.7 us
  Pallas kernels: 0 us -> 62.5 us
  matrix products: 46 us -> 0 us
  starting transfers between devices: 0.68 us -> 33.8 us
  local copies, waits for them, and re-layouts: 33.1 us -> 4.34 us
  other arithmetic: 40.7 us -> 13.1 us
  blocking collectives: 17 us -> 0 us
  between operations: 14.3 us -> 1.03 us
    reduce_scatter x5 -> x0, waiting for transfers between devices: 152 us -> none  [the longest x1 55.6 us: per_device(): lax.psum_scatter(part_grad.astype(jnp.bfloat16), 'expert', scatter_dimens...]
    ppermute x0 -> x32, waiting for transfers between devices: none -> 68.7 us  [the longest x24 34.7 us: flip(): return lax.ppermute(array, 'expert', [(i, i ^ bit) for i in range(group)])]
    pallas_call x0 -> x10, Pallas kernels: none -> 62.5 us  [the longest x4 24.6 us: rows_out(): pl.pallas_call(functools.partial(rows_kernel, blocks, len(added)), out_sh...]
    dot_general x9 -> x0, matrix products: 46 us -> none  [the longest x1 7.32 us: expert_rows(): lax.dot_general(out_grads, down_panel, (((1,), (1,)), ((), ())), preferre...]
    ppermute x0 -> x32, starting transfers between devices: none -> 33.8 us  [the longest x8 18.6 us: line_terms(): move = lambda a, pairs: lax.ppermute(a, 'dp', pairs)]
    gather x3 -> x0, local copies, waits for them, and re-layouts: 32.2 us -> none  [the longest x1 11.6 us: per_device(): inputs = all_rows[flat_row] * keep_b[:, None]]
    all_gather x2 -> x0, waiting for transfers between devices: 29.3 us -> none  [the longest x1 17.2 us: per_device(): lax.all_gather(cotangent, 'expert', axis=0, tiled=True)]
    scatter x2 -> x0, other arithmetic: 21.9 us -> none  [the longest x1 10.9 us: per_device(): part_grad = jnp.zeros((group_size * tok_dev, model_width), jnp.float32).a...]
  transfers between devices with their start and end apart: 7 -> 32, of which waited for: 6 -> 7; matrix products, arithmetic and copies ran while one was open for 29% -> 5% of each run, Pallas kernels for 0% -> 22%
where the time goes in v1:
time: 184 us; the launch traced here: 183 us
  waiting for transfers between devices  68.7 us (37%)
  Pallas kernels  62.5 us (34%)
  starting transfers between devices  33.8 us (18%)
  other arithmetic  13.1 us (7%)
  local copies, waits for them, and re-layouts  4.34 us (2%)
    ppermute x24, waiting for transfers between devices, flip(): return lax.ppermute(array, 'expert', [(i, i ^ bit) for i in range(group)])  34.7 us
    ppermute x8, waiting for transfers between devices, line_terms(): move = lambda a, pairs: lax.ppermute(a, 'dp', pairs)  33.9 us
    pallas_call x4, Pallas kernels, rows_out(): pl.pallas_call(functools.partial(rows_kernel, blocks, len(added)), out_sh...  24.6 us
    ppermute x8, starting transfers between devices, line_terms(): move = lambda a, pairs: lax.ppermute(a, 'dp', pairs)  18.6 us
    pallas_call x2, Pallas kernels, hidden(): pl.pallas_call(functools.partial(hidden_kernel, blocks), out_shape=outs,...  15.4 us
    ppermute x24, starting transfers between devices, flip(): return lax.ppermute(array, 'expert', [(i, i ^ bit) for i in range(group)])  15.1 us
    pallas_call x2, Pallas kernels, wide_grads(): pl.pallas_call(functools.partial(wide_grad_kernel, groups, first, count),...  11.8 us
    pallas_call x1, Pallas kernels, down_grads(): pl.pallas_call(functools.partial(down_grad_kernel, len(acts)), out_shape=...  6.33 us
  transfers between devices with their start and end apart: 32, of which 7 were waited for; matrix products, arithmetic and copies ran while one was open for 5% of the time, Pallas kernels for 22%

profile of v1, /device:TPU:10, one launch (start us, length us, event | category | flops | bytes accessed | tf_op | source)
XLA Modules:
  0.0 183.5 jit_solution(10120572367156926378)
XLA Ops:
  3.9 1.5 collective-permute-start.5
  5.4 1.5 collective-permute-start.6
  7.4 21.5 %collective-permute-done.5.refs_8_ = bf16[128,2048]{1,0:T(8,128)(2,1)S(1)} collective-permute-done((bf16[128,2048]{1,0:T(8,128)(2,1)}, bf16[128,2048]{1,0:T(8,128)(2,1)S(1)}, u32[]{:S(2)}, u32[]{:S(2)}) %collective-permute-start.5) | collective-permute-done | bytes 524320 | tf_op jit(solution)/shard_map/ppermute | solution.py:293
  29.0 1.6 collective-permute-start.10
  31.8 12.3 %collective-permute-done.10.refs_1_.refs_6_ = bf16[128,2176]{1,0:T(8,128)(2,1)} collective-permute-done((bf16[128,2176]{1,0:T(8,128)(2,1)S(1)}, bf16[128,2176]{1,0:T(8,128)(2,1)}, u32[]{:S(2)}, u32[]{:S(2)}) %collective-permute-start.10) | collective-permute-done | bytes 557088 | tf_op jit(solution)/shard_map/ppermute | solution.py:293
  48.2 9.8 %shard_map.119 = (bf16[768,384]{1,0:T(8,128)(2,1)}, bf16[768,768]{1,0:T(8,128)(2,1)}, bf16[384,768]{1,0:T(8,128)(2,1)}, bf16[768,768]{1,0:T(8,128)(2,1)}, bf16[768,2048]{1,0:T(8,128)(2,1)}) custom-call(s32[1]{0:T(128)} %bitcast.refs_0_, bf16[128,2176]{1,0:T(8,128)(2,1)} %copy-done, bf16[128,2176]{1,0:T(8,128)(2,1)} %copy-done.1, ...), custom_call_target="tpu_custom_call" | custom-call | flops 56623104 | bytes 279552 | tf_op jit(solution)/shard_map/pallas_call | solution.py:86
  58.1 5.6 %shard_map.120 = (bf16[256,384]{1,0:T(8,128)(2,1)}, bf16[256,768]{1,0:T(8,128)(2,1)}, bf16[384,256]{1,0:T(8,128)(2,1)}, bf16[768,256]{1,0:T(8,128)(2,1)}, bf16[256,2048]{1,0:T(8,128)(2,1)}) custom-call(s32[1]{0:T(128)} %bitcast.refs_0_, bf16[128,2176]{1,0:T(8,128)(2,1)} %collective-permute-done.10.refs_1_.refs_6_, ...), custom_call_target="tpu_custom_call" | custom-call | flops 18874368 | bytes 142336 | tf_op jit(solution)/shard_map/pallas_call | solution.py:86
  63.7 4.3 %shard_map.121 = bf16[768,512]{1,0:T(8,128)(2,1)} custom-call(s32[4]{0:T(128)} %dynamic-slice_bitcast_fusion.order_ref, bf16[128,2176]{1,0:T(8,128)(2,1)} %copy-done, bf16[128,2176]{1,0:T(8,128)(2,1)} %copy-done.1, bf16[128,2176]{1,0:T(8,128)(2,1)} %copy-done.2, bf16[128,2176]{1,0:T(8,128)(2,1)} %copy-done.3, bf16[128,2176]{1,0:T(8,128)(2,1)} %copy-done.4, ...), custom_call_target="tpu_custom_call" | custom-call | flops 12582912 | bytes 36864 | tf_op jit(solution)/shard_map/pallas_call | solution.py:190
  68.0 6.3 %shard_map.122 = (bf16[96,2048]{1,0:T(8,128)(2,1)}, bf16[96,2048]{1,0:T(8,128)(2,1)}, bf16[96,2048]{1,0:T(8,128)(2,1)}, bf16[96,2048]{1,0:T(8,128)(2,1)}) custom-call(s32[4]{0:T(128)} %dynamic-slice_bitcast_fusion.order_ref, bf16[384,768]{1,0:T(8,128)(2,1)} %get-tuple-element.50.refs_0_, bf16[384,256]{1,0:T(8,128)(2,1)} %get-tuple-element.51.refs_1_, ...), custom_call_target="tpu_custom_call" | custom-call | flops 25165824 | bytes 77824 | tf_op jit(solution)/shard_map/pallas_call | solution.py:224
  74.3 5.4 %shard_map.123 = (bf16[128,2048]{1,0:T(8,128)(2,1)}, bf16[128,2048]{1,0:T(8,128)(2,1)}) custom-call(s32[1]{0:T(128)} %bitcast.refs_0_, bf16[128,2176]{1,0:T(8,128)(2,1)} %collective-permute-done.11.refs_2_.refs_7_.refs_1_, bf16[256,384]{1,0:T(8,128)(2,1)} %get-tuple-element.55.refs_2_, bf16[256,768]{1,0:T(8,128)(2,1)} %get-tuple-element.56.refs_3_, ...), custom_call_target="tpu_custom_call" | custom-call | flops 9437184 | bytes 90112 | tf_op jit(solution)/shard_map/pallas_call | solution.py:147
  80.7 1.6 collective-permute-start.24
  82.3 7.5 %shard_map.124 = (bf16[768,512]{1,0:T(8,128)(2,1)}, bf16[768,512]{1,0:T(8,128)(2,1)}, bf16[768,512]{1,0:T(8,128)(2,1)}) custom-call(s32[4]{0:T(128)} %dynamic-slice_bitcast_fusion.order_ref, bf16[128,2176]{1,0:T(8,128)(2,1)} %copy-done, bf16[128,2176]{1,0:T(8,128)(2,1)} %copy-done.1, bf16[128,2176]{1,0:T(8,128)(2,1)} %copy-done.2, ...), custom_call_target="tpu_custom_call" | custom-call | flops 37748736 | bytes 61440 | tf_op jit(solution)/shard_map/pallas_call | solution.py:190
  90.8 5.7 %shard_map.125 = (bf16[128,2048]{1,0:T(8,128)(2,1)}, bf16[128,2048]{1,0:T(8,128)(2,1)}) custom-call(s32[1]{0:T(128)} %bitcast.refs_0_, bf16[128,2176]{1,0:T(8,128)(2,1)} %collective-permute-done.10.refs_1_.refs_6_, bf16[256,384]{1,0:T(8,128)(2,1)} %get-tuple-element.55.refs_2_, bf16[256,768]{1,0:T(8,128)(2,1)} %get-tuple-element.56.refs_3_, ...), custom_call_target="tpu_custom_call" | custom-call | flops 9437184 | bytes 106496 | tf_op jit(solution)/shard_map/pallas_call | solution.py:147
  96.5 6.3 %shard_map.126 = (bf16[384,2048]{1,0:T(8,128)(2,1)}, bf16[384,2048]{1,0:T(8,128)(2,1)}) custom-call(s32[1]{0:T(128)} %bitcast.refs_0_, bf16[128,2176]{1,0:T(8,128)(2,1)} %copy-done.3, bf16[128,2176]{1,0:T(8,128)(2,1)} %copy-done.4, bf16[128,2176]{1,0:T(8,128)(2,1)} %copy-done.5, bf16[768,384]{1,0:T(8,128)(2,1)} %get-tuple-element.65.refs_4_, ...), custom_call_target="tpu_custom_call" | custom-call | flops 28311552 | bytes 122880 | tf_op jit(solution)/shard_map/pallas_call | solution.py:147
  104.2 2.6 %collective-permute-start.30 = (bf16[96,2048]{1,0:T(8,128)(2,1)}, bf16[96,2048]{1,0:T(8,128)(2,1)S(1)}, u32[]{:S(2)}, u32[]{:S(2)}) collective-permute-start(bf16[96,2048]{1,0:T(8,128)(2,1)} %add_convert_fusion.6), channel_id=1, source_target_pairs={{0,8},{8,24},{24,16},{16,0},{1,9},{9,25},{25,17},{17,1},{2,10},{10... | collective-permute-start | bytes 1179656 | tf_op jit(solution)/shard_map/ppermute | solution.py:272
  106.8 16.6 %collective-permute-done.24.a1 = bf16[768,512]{1,0:T(8,128)(2,1)S(1)} collective-permute-done((bf16[768,512]{1,0:T(8,128)(2,1)S(1)}, bf16[768,512]{1,0:T(8,128)(2,1)S(1)}, u32[]{:S(2)}, u32[]{:S(2)}) %collective-permute-start.24) | collective-permute-done | bytes 786464 | tf_op jit(solution)/shard_map/ppermute | solution.py:272
  123.6 4.6 %collective-permute-start.25 = (bf16[768,512]{1,0:T(8,128)(2,1)S(1)}, bf16[768,512]{1,0:T(8,128)(2,1)S(1)}, u32[]{:S(2)}, u32[]{:S(2)}) collective-permute-start(bf16[768,512]{1,0:T(8,128)(2,1)S(1)} %add_convert_fusion.1), channel_id=1, source_target_pairs={{0,8},{8,24},{24,16},{16,0},{1,9},{9,25},{25,17},{17,1},{2,10},{10... | collective-permute-start | bytes 2359304 | tf_op jit(solution)/shard_map/ppermute | solution.py:272
  128.2 1.4 collective-permute-start.26
  131.1 13.4 %collective-permute-done.25.a2 = bf16[768,512]{1,0:T(8,128)(2,1)S(1)} collective-permute-done((bf16[768,512]{1,0:T(8,128)(2,1)S(1)}, bf16[768,512]{1,0:T(8,128)(2,1)S(1)}, u32[]{:S(2)}, u32[]{:S(2)}) %collective-permute-start.25) | collective-permute-done | bytes 786464 | tf_op jit(solution)/shard_map/ppermute | solution.py:272
  144.6 1.5 collective-permute-start.22
  146.3 1.3 collective-permute-start.28
  147.6 4.6 %collective-permute-start.31 = (bf16[96,2048]{1,0:T(8,128)(2,1)}, bf16[96,2048]{1,0:T(8,128)(2,1)}, u32[]{:S(2)}, u32[]{:S(2)}) collective-permute-start(bf16[96,2048]{1,0:T(8,128)(2,1)} %fusion), channel_id=1, source_target_pairs={{8,16},{16,8},{9,17},{17,9},{10,18},{18,10},{11,19},{19,11},{12,20... | collective-permute-start | bytes 1179656 | tf_op jit(solution)/shard_map/ppermute | solution.py:272
  152.2 7.3 %shard_map.127 = (bf16[128,2048]{1,0:T(8,128)(2,1)}, bf16[128,2048]{1,0:T(8,128)(2,1)}, bf16[128,2048]{1,0:T(8,128)(2,1)}, bf16[128,2048]{1,0:T(8,128)(2,1)}, bf...) custom-call(s32[1]{0:T(128)} %bitcast.refs_0_, bf16[128,2176]{1,0:T(8,128)(2,1)} %copy-done, ...), custom_call_target="tpu_custom_call" | custom-call | flops 28311552 | bytes 172032 | tf_op jit(solution)/shard_map/pallas_call | solution.py:147
  159.5 2.1 %collective-permute-start.27 = (bf16[768,512]{1,0:T(8,128)(2,1)S(1)}, bf16[768,512]{1,0:T(8,128)(2,1)S(1)}, u32[]{:S(2)}, u32[]{:S(2)}) collective-permute-start(bf16[768,512]{1,0:T(8,128)(2,1)S(1)} %add_convert_fusion), channel_id=1, source_target_pairs={{8,16},{16,8},{9,17},{17,9},{10,18},{18,10},{11,19},{19,11},{12,20... | collective-permute-start | bytes 2359304 | tf_op jit(solution)/shard_map/ppermute | solution.py:272
  161.6 1.4 add_convert_fusion.5
  164.2 1.6 collective-permute-start.23
  165.8 1.5 collective-permute-start.21
  167.3 2.3 %fusion.3 = f32[1,96,2048]{2,1,0:T(8,128)} fusion(bf16[96,2048]{1,0:T(8,128)(2,1)S(1)} %collective-permute-done.30, bf16[96,2048]{1,0:T(8,128)(2,1)S(1)} %collective-permute-done.29, bf16[96,2048]{1,0:T(8,128)(2,1)} %collective-permute-done.31, bf16[96,2048]{1,0:T(8,128)(2,1)} %collective-permute-done.28, bf16[96,2048]{1,0:T(8,128)(2,1)S(1)} %copy-done.22, ...), kind=kLoop, calls=%fused_computation.11 | loop fusion | flops 1966080 | bytes 2752513 | tf_op jit(solution)/shard_map/broadcast_in_dim | solution.py:349
  169.6 3.9 %collective-permute-done.27.a4 = bf16[768,512]{1,0:T(8,128)(2,1)S(1)} collective-permute-done((bf16[768,512]{1,0:T(8,128)(2,1)S(1)}, bf16[768,512]{1,0:T(8,128)(2,1)S(1)}, u32[]{:S(2)}, u32[]{:S(2)}) %collective-permute-start.27) | collective-permute-done | bytes 786464 | tf_op jit(solution)/shard_map/ppermute | solution.py:272
  174.5 4.4 %shard_map.128 = (f32[512,384]{1,0:T(8,128)}, f32[512,384]{1,0:T(8,128)}) custom-call(s32[1]{0:T(128)} %bitcast.5.mid_ref, bf16[768,512]{1,0:T(8,128)(2,1)} %get-tuple-element.76.own, bf16[768,512]{1,0:T(8,128)(2,1)} %copy-done.6, bf16[768,512]{1,0:T(8,128)(2,1)} %copy-done.7, bf16[768,512]{1,0:T(8,128)(2,1)} %collective-permute-done.26.a3, ...), custom_call_target="tpu_custom_call" | custom-call | flops 30720 | bytes 86016 | tf_op jit(solution)/shard_map/pallas_call | solution.py:252
  178.9 2.3 %add_convert_fusion.4 = bf16[128,2048]{1,0:T(8,128)(2,1)} fusion(bf16[128,2048]{1,0:T(8,128)(2,1)} %collective-permute-done.20, bf16[128,2048]{1,0:T(8,128)(2,1)} %collective-permute-done.18, bf16[128,2048]{1,0:T(8,128)(2,1)S(1)} %copy-done.17), kind=kLoop, calls=%fused_computation.4 | loop fusion | flops 1572864 | bytes 2097152 | tf_op jit(solution)/shard_map/convert_element_type | solution.py:349
  181.2 2.2 %add_convert_fusion.2 = bf16[128,2048]{1,0:T(8,128)(2,1)} fusion(bf16[128,2048]{1,0:T(8,128)(2,1)} %collective-permute-done.23, bf16[128,2048]{1,0:T(8,128)(2,1)} %collective-permute-done.21, bf16[128,2048]{1,0:T(8,128)(2,1)S(1)} %copy-done.16), kind=kLoop, calls=%fused_computation.2 | loop fusion | flops 1572864 | bytes 2097152 | tf_op jit(solution)/shard_map/convert_element_type | solution.py:349
  (101 shorter events, 16.5 us)
Async XLA Ops:
  3.3 25.7 %collective-permute-start = (bf16[128,2176]{1,0:T(8,128)(2,1)S(1)}, bf16[128,2176]{1,0:T(8,128)(2,1)S(1)}, u32[]{:S(2)}, u32[]{:S(2)}) collective-permute-start(bf16[128,2176]{1,0:T(8,128)(2,1)S(1)} %pad_maximum_fusion.refs_1_.refs_0_), channel_id=1, source_target_pairs={{0,2},{1,3},{2,0},{3,1},{4,6},{5,7},{6,4},{7,5},{8,10},{9,11},{10,... | collective-permute-start | bytes 1671176 | tf_op jit(solution)/shard_map/ppermute | solution.py:293
  3.9 25.1 %collective-permute-start.5 = (bf16[128,2048]{1,0:T(8,128)(2,1)}, bf16[128,2048]{1,0:T(8,128)(2,1)S(1)}, u32[]{:S(2)}, u32[]{:S(2)}) collective-permute-start(bf16[128,2048]{1,0:T(8,128)(2,1)} %refs_7_.1), channel_id=1, source_target_pairs={{0,2},{1,3},{2,0},{3,1},{4,6},{5,7},{6,4},{7,5},{8,10},{9,11},{10,... | collective-permute-start | bytes 1572872 | tf_op jit(solution)/shard_map/ppermute | solution.py:293
  5.4 25.2 %collective-permute-start.6 = (bf16[128,2048]{1,0:T(8,128)(2,1)}, bf16[128,2048]{1,0:T(8,128)(2,1)}, u32[]{:S(2)}, u32[]{:S(2)}) collective-permute-start(bf16[128,2048]{1,0:T(8,128)(2,1)} %refs_7_.1), channel_id=1, source_target_pairs={{0,4},{1,5},{2,6},{3,7},{4,0},{5,1},{6,2},{7,3},{8,12},{9,13},{10,... | collective-permute-start | bytes 1572872 | tf_op jit(solution)/shard_map/ppermute | solution.py:293
  6.9 23.8 %collective-permute-start.7 = (bf16[128,2048]{1,0:T(8,128)(2,1)}, bf16[128,2048]{1,0:T(8,128)(2,1)S(1)}, u32[]{:S(2)}, u32[]{:S(2)}) collective-permute-start(bf16[128,2048]{1,0:T(8,128)(2,1)} %refs_7_.1), channel_id=1, source_target_pairs={{0,1},{1,0},{2,3},{3,2},{4,5},{5,4},{6,7},{7,6},{8,9},{9,8},{10,11... | collective-permute-start | bytes 1572872 | tf_op jit(solution)/shard_map/ppermute | solution.py:293
  6.9 24.4 %collective-permute-start.1 = (bf16[128,2176]{1,0:T(8,128)(2,1)S(1)}, bf16[128,2176]{1,0:T(8,128)(2,1)S(1)}, u32[]{:S(2)}, u32[]{:S(2)}) collective-permute-start(bf16[128,2176]{1,0:T(8,128)(2,1)S(1)} %pad_maximum_fusion.refs_1_.refs_0_), channel_id=1, source_target_pairs={{0,4},{1,5},{2,6},{3,7},{4,0},{5,1},{6,2},{7,3},{8,12},{9,13},{10,... | collective-permute-start | bytes 1671176 | tf_op jit(solution)/shard_map/ppermute | solution.py:293
  29.0 2.4 %collective-permute-start.2 = (bf16[128,2176]{1,0:T(8,128)(2,1)S(1)}, bf16[128,2176]{1,0:T(8,128)(2,1)S(1)}, u32[]{:S(2)}, u32[]{:S(2)}) collective-permute-start(bf16[128,2176]{1,0:T(8,128)(2,1)S(1)} %pad_maximum_fusion.refs_1_.refs_0_), channel_id=1, source_target_pairs={{0,1},{1,0},{2,3},{3,2},{4,5},{5,4},{6,7},{7,6},{8,9},{9,8},{10,11... | collective-permute-start | bytes 1671176 | tf_op jit(solution)/shard_map/ppermute | solution.py:293
  29.0 15.1 %collective-permute-start.10 = (bf16[128,2176]{1,0:T(8,128)(2,1)S(1)}, bf16[128,2176]{1,0:T(8,128)(2,1)}, u32[]{:S(2)}, u32[]{:S(2)}) collective-permute-start(bf16[128,2176]{1,0:T(8,128)(2,1)S(1)} %collective-permute-done.refs_2_.refs_1_), channel_id=1, source_target_pairs={{0,4},{1,5},{2,6},{3,7},{4,0},{5,1},{6,2},{7,3},{8,12},{9,13},{10,... | collective-permute-start | bytes 1671176 | tf_op jit(solution)/shard_map/ppermute | solution.py:293
  30.6 13.6 %collective-permute-start.8 = (bf16[128,2048]{1,0:T(8,128)(2,1)S(1)}, bf16[128,2048]{1,0:T(8,128)(2,1)S(1)}, u32[]{:S(2)}, u32[]{:S(2)}) collective-permute-start(bf16[128,2048]{1,0:T(8,128)(2,1)S(1)} %collective-permute-done.5.refs_8_), channel_id=1, source_target_pairs={{0,1},{1,0},{2,3},{3,2},{4,5},{5,4},{6,7},{7,6},{8,9},{9,8},{10,11... | collective-permute-start | bytes 1572872 | tf_op jit(solution)/shard_map/ppermute | solution.py:293
  30.8 14.5 %collective-permute-start.12 = (bf16[128,2048]{1,0:T(8,128)(2,1)}, bf16[128,2048]{1,0:T(8,128)(2,1)}, u32[]{:S(2)}, u32[]{:S(2)}) collective-permute-start(bf16[128,2048]{1,0:T(8,128)(2,1)} %collective-permute-done.6.refs_9_), channel_id=1, source_target_pairs={{0,2},{1,3},{2,0},{3,1},{4,6},{5,7},{6,4},{7,5},{8,10},{9,11},{10,... | collective-permute-start | bytes 1572872 | tf_op jit(solution)/shard_map/ppermute | solution.py:293
  31.3 15.9 %collective-permute-start.3 = (bf16[128,2176]{1,0:T(8,128)(2,1)S(1)}, bf16[128,2176]{1,0:T(8,128)(2,1)S(1)}, u32[]{:S(2)}, u32[]{:S(2)}) collective-permute-start(bf16[128,2176]{1,0:T(8,128)(2,1)S(1)} %collective-permute-done.refs_2_.refs_1_), channel_id=1, source_target_pairs={{0,1},{1,0},{2,3},{3,2},{4,5},{5,4},{6,7},{7,6},{8,9},{9,8},{10,11... | collective-permute-start | bytes 1671176 | tf_op jit(solution)/shard_map/ppermute | solution.py:293
  31.4 15.8 %collective-permute-start.4 = (bf16[128,2176]{1,0:T(8,128)(2,1)S(1)}, bf16[128,2176]{1,0:T(8,128)(2,1)S(1)}, u32[]{:S(2)}, u32[]{:S(2)}) collective-permute-start(bf16[128,2176]{1,0:T(8,128)(2,1)S(1)} %collective-permute-done.1.refs_3_.refs_2_), channel_id=1, source_target_pairs={{0,1},{1,0},{2,3},{3,2},{4,5},{5,4},{6,7},{7,6},{8,9},{9,8},{10,11... | collective-permute-start | bytes 1671176 | tf_op jit(solution)/shard_map/ppermute | solution.py:293
  44.1 13.9 %collective-permute-start.11 = (bf16[128,2176]{1,0:T(8,128)(2,1)}, bf16[128,2176]{1,0:T(8,128)(2,1)}, u32[]{:S(2)}, u32[]{:S(2)}) collective-permute-start(bf16[128,2176]{1,0:T(8,128)(2,1)} %collective-permute-done.10.refs_1_.refs_6_), channel_id=1, source_target_pairs={{0,1},{1,0},{2,3},{3,2},{4,5},{5,4},{6,7},{7,6},{8,9},{9,8},{10,11... | collective-permute-start | bytes 1671176 | tf_op jit(solution)/shard_map/ppermute | solution.py:293
  44.2 3.0 %collective-permute-start.9 = (bf16[128,2048]{1,0:T(8,128)(2,1)}, bf16[128,2048]{1,0:T(8,128)(2,1)}, u32[]{:S(2)}, u32[]{:S(2)}) collective-permute-start(bf16[128,2048]{1,0:T(8,128)(2,1)} %collective-permute-done.6.refs_9_), channel_id=1, source_target_pairs={{0,1},{1,0},{2,3},{3,2},{4,5},{5,4},{6,7},{7,6},{8,9},{9,8},{10,11... | collective-permute-start | bytes 1572872 | tf_op jit(solution)/shard_map/ppermute | solution.py:293
  45.2 12.8 %collective-permute-start.13 = (bf16[128,2048]{1,0:T(8,128)(2,1)}, bf16[128,2048]{1,0:T(8,128)(2,1)}, u32[]{:S(2)}, u32[]{:S(2)}) collective-permute-start(bf16[128,2048]{1,0:T(8,128)(2,1)} %collective-permute-done.12.refs_3_), channel_id=1, source_target_pairs={{0,1},{1,0},{2,3},{3,2},{4,5},{5,4},{6,7},{7,6},{8,9},{9,8},{10,11... | collective-permute-start | bytes 1572872 | tf_op jit(solution)/shard_map/ppermute | solution.py:293
  79.7 10.1 %collective-permute-start.14 = (bf16[128,2048]{1,0:T(8,128)(2,1)}, bf16[128,2048]{1,0:T(8,128)(2,1)S(1)}, u32[]{:S(2)}, u32[]{:S(2)}) collective-permute-start(bf16[128,2048]{1,0:T(8,128)(2,1)} %get-tuple-element.57), channel_id=1, source_target_pairs={{0,1},{1,0},{2,3},{3,2},{4,5},{5,4},{6,7},{7,6},{8,9},{9,8},{10,11... | collective-permute-start | bytes 1572872 | tf_op jit(solution)/shard_map/ppermute | solution.py:293
  79.9 9.9 %collective-permute-start.15 = (bf16[128,2048]{1,0:T(8,128)(2,1)}, bf16[128,2048]{1,0:T(8,128)(2,1)S(1)}, u32[]{:S(2)}, u32[]{:S(2)}) collective-permute-start(bf16[128,2048]{1,0:T(8,128)(2,1)} %get-tuple-element.58), channel_id=1, source_target_pairs={{0,1},{1,0},{2,3},{3,2},{4,5},{5,4},{6,7},{7,6},{8,9},{9,8},{10,11... | collective-permute-start | bytes 1572872 | tf_op jit(solution)/shard_map/ppermute | solution.py:293
  80.3 23.0 %collective-permute-start.29 = (bf16[96,2048]{1,0:T(8,128)(2,1)}, bf16[96,2048]{1,0:T(8,128)(2,1)S(1)}, u32[]{:S(2)}, u32[]{:S(2)}) collective-permute-start(bf16[96,2048]{1,0:T(8,128)(2,1)} %get-tuple-element.54), channel_id=1, source_target_pairs={{0,8},{8,0},{16,24},{24,16},{1,9},{9,1},{17,25},{25,17},{2,10},{10... | collective-permute-start | bytes 1179656 | tf_op jit(solution)/shard_map/ppermute | solution.py:272
  80.7 42.6 %collective-permute-start.24 = (bf16[768,512]{1,0:T(8,128)(2,1)S(1)}, bf16[768,512]{1,0:T(8,128)(2,1)S(1)}, u32[]{:S(2)}, u32[]{:S(2)}) collective-permute-start(bf16[768,512]{1,0:T(8,128)(2,1)S(1)} %copy-done.11), channel_id=1, source_target_pairs={{0,8},{8,0},{16,24},{24,16},{1,9},{9,1},{17,25},{25,17},{2,10},{10... | collective-permute-start | bytes 2359304 | tf_op jit(solution)/shard_map/ppermute | solution.py:272
  102.7 43.6 %collective-permute-start.16 = (bf16[384,2048]{1,0:T(8,128)(2,1)}, bf16[384,2048]{1,0:T(8,128)(2,1)}, u32[]{:S(2)}, u32[]{:S(2)}) collective-permute-start(bf16[384,2048]{1,0:T(8,128)(2,1)} %get-tuple-element.67), channel_id=1, source_target_pairs={{0,1},{1,0},{2,3},{3,2},{4,5},{5,4},{6,7},{7,6},{8,9},{9,8},{10,11... | collective-permute-start | bytes 4718600 | tf_op jit(solution)/shard_map/ppermute | solution.py:293
  102.8 44.8 %collective-permute-start.17 = (bf16[384,2048]{1,0:T(8,128)(2,1)}, bf16[384,2048]{1,0:T(8,128)(2,1)}, u32[]{:S(2)}, u32[]{:S(2)}) collective-permute-start(bf16[384,2048]{1,0:T(8,128)(2,1)} %get-tuple-element.68), channel_id=1, source_target_pairs={{0,1},{1,0},{2,3},{3,2},{4,5},{5,4},{6,7},{7,6},{8,9},{9,8},{10,11... | collective-permute-start | bytes 4718600 | tf_op jit(solution)/shard_map/ppermute | solution.py:293
  104.2 25.5 %collective-permute-start.30 = (bf16[96,2048]{1,0:T(8,128)(2,1)}, bf16[96,2048]{1,0:T(8,128)(2,1)S(1)}, u32[]{:S(2)}, u32[]{:S(2)}) collective-permute-start(bf16[96,2048]{1,0:T(8,128)(2,1)} %add_convert_fusion.6), channel_id=1, source_target_pairs={{0,8},{8,24},{24,16},{16,0},{1,9},{9,25},{25,17},{17,1},{2,10},{10... | collective-permute-start | bytes 1179656 | tf_op jit(solution)/shard_map/ppermute | solution.py:272
  123.6 21.0 %collective-permute-start.25 = (bf16[768,512]{1,0:T(8,128)(2,1)S(1)}, bf16[768,512]{1,0:T(8,128)(2,1)S(1)}, u32[]{:S(2)}, u32[]{:S(2)}) collective-permute-start(bf16[768,512]{1,0:T(8,128)(2,1)S(1)} %add_convert_fusion.1), channel_id=1, source_target_pairs={{0,8},{8,24},{24,16},{16,0},{1,9},{9,25},{25,17},{17,1},{2,10},{10... | collective-permute-start | bytes 2359304 | tf_op jit(solution)/shard_map/ppermute | solution.py:272
  128.2 36.0 %collective-permute-start.26 = (bf16[768,512]{1,0:T(8,128)(2,1)}, bf16[768,512]{1,0:T(8,128)(2,1)}, u32[]{:S(2)}, u32[]{:S(2)}) collective-permute-start(bf16[768,512]{1,0:T(8,128)(2,1)} %get-tuple-element.77), channel_id=1, source_target_pairs={{0,8},{24,16},{1,9},{25,17},{2,10},{26,18},{3,11},{27,19},{4,12},{... | collective-permute-start | bytes 2359304 | tf_op jit(solution)/shard_map/ppermute | solution.py:272
  129.7 29.9 %collective-permute-start.19 = (bf16[128,2048]{1,0:T(8,128)(2,1)}, bf16[128,2048]{1,0:T(8,128)(2,1)}, u32[]{:S(2)}, u32[]{:S(2)}) collective-permute-start(bf16[128,2048]{1,0:T(8,128)(2,1)} %get-tuple-element.64), channel_id=1, source_target_pairs={{0,2},{1,3},{2,0},{3,1},{4,6},{5,7},{6,4},{7,5},{8,10},{9,11},{10,... | collective-permute-start | bytes 1572872 | tf_op jit(solution)/shard_map/ppermute | solution.py:293
  144.6 19.0 %collective-permute-start.22 = (bf16[128,2048]{1,0:T(8,128)(2,1)}, bf16[128,2048]{1,0:T(8,128)(2,1)S(1)}, u32[]{:S(2)}, u32[]{:S(2)}) collective-permute-start(bf16[128,2048]{1,0:T(8,128)(2,1)} %get-tuple-element.75), channel_id=1, source_target_pairs={{0,4},{1,5},{2,6},{3,7},{4,0},{5,1},{6,2},{7,3},{8,12},{9,13},{10,... | collective-permute-start | bytes 1572872 | tf_op jit(solution)/shard_map/ppermute | solution.py:293
  146.3 16.7 %collective-permute-start.28 = (bf16[96,2048]{1,0:T(8,128)(2,1)S(1)}, bf16[96,2048]{1,0:T(8,128)(2,1)}, u32[]{:S(2)}, u32[]{:S(2)}) collective-permute-start(bf16[96,2048]{1,0:T(8,128)(2,1)S(1)} %copy-done.20), channel_id=1, source_target_pairs={{0,8},{24,16},{1,9},{25,17},{2,10},{26,18},{3,11},{27,19},{4,12},{... | collective-permute-start | bytes 1179656 | tf_op jit(solution)/shard_map/ppermute | solution.py:272
  147.6 18.2 %collective-permute-start.31 = (bf16[96,2048]{1,0:T(8,128)(2,1)}, bf16[96,2048]{1,0:T(8,128)(2,1)}, u32[]{:S(2)}, u32[]{:S(2)}) collective-permute-start(bf16[96,2048]{1,0:T(8,128)(2,1)} %fusion), channel_id=1, source_target_pairs={{8,16},{16,8},{9,17},{17,9},{10,18},{18,10},{11,19},{19,11},{12,20... | collective-permute-start | bytes 1179656 | tf_op jit(solution)/shard_map/ppermute | solution.py:272
  159.5 14.0 %collective-permute-start.27 = (bf16[768,512]{1,0:T(8,128)(2,1)S(1)}, bf16[768,512]{1,0:T(8,128)(2,1)S(1)}, u32[]{:S(2)}, u32[]{:S(2)}) collective-permute-start(bf16[768,512]{1,0:T(8,128)(2,1)S(1)} %add_convert_fusion), channel_id=1, source_target_pairs={{8,16},{16,8},{9,17},{17,9},{10,18},{18,10},{11,19},{19,11},{12,20... | collective-permute-start | bytes 2359304 | tf_op jit(solution)/shard_map/ppermute | solution.py:272
  163.0 15.9 %collective-permute-start.20 = (bf16[128,2048]{1,0:T(8,128)(2,1)S(1)}, bf16[128,2048]{1,0:T(8,128)(2,1)}, u32[]{:S(2)}, u32[]{:S(2)}) collective-permute-start(bf16[128,2048]{1,0:T(8,128)(2,1)S(1)} %add_convert_fusion.5), channel_id=1, source_target_pairs={{0,4},{1,5},{2,6},{3,7},{4,0},{5,1},{6,2},{7,3},{8,12},{9,13},{10,... | collective-permute-start | bytes 1572872 | tf_op jit(solution)/shard_map/ppermute | solution.py:293
  163.6 15.3 %collective-permute-start.18 = (bf16[128,2048]{1,0:T(8,128)(2,1)}, bf16[128,2048]{1,0:T(8,128)(2,1)}, u32[]{:S(2)}, u32[]{:S(2)}) collective-permute-start(bf16[128,2048]{1,0:T(8,128)(2,1)} %get-tuple-element.70), channel_id=1, source_target_pairs={{0,2},{1,3},{2,0},{3,1},{4,6},{5,7},{6,4},{7,5},{8,10},{9,11},{10,... | collective-permute-start | bytes 1572872 | tf_op jit(solution)/shard_map/ppermute | solution.py:293
  164.2 17.0 %collective-permute-start.23 = (bf16[128,2048]{1,0:T(8,128)(2,1)S(1)}, bf16[128,2048]{1,0:T(8,128)(2,1)}, u32[]{:S(2)}, u32[]{:S(2)}) collective-permute-start(bf16[128,2048]{1,0:T(8,128)(2,1)S(1)} %add_convert_fusion.3), channel_id=1, source_target_pairs={{0,2},{1,3},{2,0},{3,1},{4,6},{5,7},{6,4},{7,5},{8,10},{9,11},{10,... | collective-permute-start | bytes 1572872 | tf_op jit(solution)/shard_map/ppermute | solution.py:293
  165.8 15.4 %collective-permute-start.21 = (bf16[128,2048]{1,0:T(8,128)(2,1)}, bf16[128,2048]{1,0:T(8,128)(2,1)}, u32[]{:S(2)}, u32[]{:S(2)}) collective-permute-start(bf16[128,2048]{1,0:T(8,128)(2,1)} %get-tuple-element.73), channel_id=1, source_target_pairs={{0,4},{1,5},{2,6},{3,7},{4,0},{5,1},{6,2},{7,3},{8,12},{9,13},{10,... | collective-permute-start | bytes 1572872 | tf_op jit(solution)/shard_map/ppermute | solution.py:293
  (23 other events, 246.4 us)

commit v2 on v1

--- a/solution.py
+++ b/solution.py
@@ -10,6 +10,7 @@
 F32 = jnp.float32
 BF16 = jnp.bfloat16
 LANES = 128
+CHUNKS = 4
 CORE, NEAR, FAR = 1, 2, 4
 PARAMS = pltpu.CompilerParams(vmem_limit_bytes=60 * 1024 * 1024)
 ANY = pl.BlockSpec(memory_space=pl.ANY)
@@ -26,6 +27,26 @@
     lane = lax.broadcasted_iota(jnp.int32, gate_rows.shape, 1)
     kept = jnp.where(lane == expert_num, gate_rows.astype(F32), 0.0)
     return jnp.sum(kept, axis=1, keepdims=True)
+
+
+def pack_kernel(tok_ref, ids_ref, gates_ref, out_ref):
+    rows, width = tok_ref.shape
+    out_ref[:, :width] = tok_ref[...]
+    lane = lax.broadcasted_iota(jnp.int32, (rows, LANES), 1)
+    ids, gates = ids_ref[...], gates_ref[...].astype(F32)
+    total = jnp.zeros((rows, LANES), F32)
+    for k in range(ids.shape[1]):
+        total = total + jnp.where(ids[:, k : k + 1] == lane, gates[:, k : k + 1], 0.0)
+    out_ref[:, width:] = total.astype(BF16)
+
+
+def packed(tokens, ids, gates):
+    rows, width = tokens.shape
+    return pl.pallas_call(
+        pack_kernel,
+        out_shape=jax.ShapeDtypeStruct((rows, width + LANES), BF16),
+        compiler_params=PARAMS,
+    )(tokens, ids, gates)
 
 
 def hidden_kernel(blocks, *refs):
@@ -42,19 +63,31 @@
         made.start()
         return made
 
-    first = [copy(wg_hbm, wide.at[:, :hid], 0), copy(wu_hbm, wide.at[:, hid:], 1)]
-    for i in range(blocks):
-        at = pl.ds(i * each, each)
-        first.append(copy(toks[i].at[:, :width], rows.at[at, :], 3 + 3 * i))
+    def at(i):
+        return pl.ds(i * each, each)
+
+    step = width // CHUNKS
+    tok_copies = [copy(toks[i].at[:, :width], rows.at[at(i), :], 3 * i) for i in range(blocks)]
+    wide_copies = []
+    for j in range(CHUNKS):
+        part = pl.ds(j * step, step)
+        number = 3 * blocks + 1 + 2 * j
+        wide_copies.append(copy(wg_hbm.at[part, :], wide.at[part, :hid], number))
+        wide_copies.append(copy(wu_hbm.at[part, :], wide.at[part, hid:], number + 1))
     second = []
     for i in range(blocks):
-        at = pl.ds(i * each, each)
-        second.append(copy(toks[i].at[:, width:], gates.at[at, :], 4 + 3 * i))
-        second.append(copy(cots[i], cot.at[at, :], 5 + 3 * i))
-    second.append(copy(wd_hbm, down, 2))
-    for made in first:
+        second.append(copy(toks[i].at[:, width:], gates.at[at(i), :], 3 * i + 1))
+        second.append(copy(cots[i], cot.at[at(i), :], 3 * i + 2))
+    second.append(copy(wd_hbm, down, 3 * blocks))
+    for made in tok_copies:
         made.wait()
-    pre = jnp.dot(rows[...], wide[...], preferred_element_type=F32)
+    pre = None
+    for j in range(CHUNKS):
+        wide_copies[2 * j].wait()
+        wide_copies[2 * j + 1].wait()
+        part = slice(j * step, (j + 1) * step)
+        more = jnp.dot(rows[:, part], wide[part, :], preferred_element_type=F32)
+        pre = more if pre is None else pre + more
     for made in second:
         made.wait()
     og[...] = (own_gate(gates[...], me_ref[0]) * cot[...].astype(F32)).astype(BF16)
@@ -96,18 +129,18 @@
             pltpu.VMEM((width, 2 * hid), BF16),
             pltpu.VMEM((hid, width), BF16),
             pltpu.VMEM((rows, width), BF16),
-            pltpu.SemaphoreType.DMA((3 + 3 * blocks,)),
+            pltpu.SemaphoreType.DMA((3 * blocks + 1 + 2 * CHUNKS,)),
         ],
         compiler_params=PARAMS,
         cost_estimate=cost(6 * rows * width * hid, (*toks, *cots, wg, wu, wd) + outs),
     )(me, *toks, *cots, wg, wu, wd)
 
 
-def rows_kernel(blocks, more, *refs):
+def rows_kernel(blocks, groups, more, *refs):
     me_ref, gates, refs = refs[0], refs[1 : 1 + blocks], refs[1 + blocks :]
-    act_ref, hid_ref, wg_hbm, wu_hbm, wd_hbm = refs[:5]
-    added = refs[5 : 5 + more]
-    outs, (wide, down, sems) = refs[5 + more : -3], refs[-3:]
+    acts, hids, refs = refs[:groups], refs[groups : 2 * groups], refs[2 * groups :]
+    wg_hbm, wu_hbm, wd_hbm = refs[:3]
+    added, outs, (wide, down, sems) = refs[3 : 3 + more], refs[3 + more : -3], refs[-3:]
     hid = wg_hbm.shape[1]
     copies = [
         pltpu.make_async_copy(wd_hbm, down, sems.at[0]),
@@ -117,51 +150,51 @@
     for made in copies:
         made.start()
     gate_col = own_gate(jnp.concatenate([g[...] for g in gates], axis=0), me_ref[0])
-    half = len(outs) // 2
+    each = gates[0].shape[0]
 
     def put(values, number):
-        if more:
-            values = values.astype(F32) + added[number][...].astype(F32)
-        values = values.astype(BF16)
-        each = values.shape[0] // half
-        for i in range(half):
-            outs[number * half + i][...] = values[i * each : (i + 1) * each]
+        for i in range(blocks):
+            piece = values[i * each : (i + 1) * each]
+            if more:
+                piece = (piece.astype(F32) + added[number * blocks + i][...].astype(F32)).astype(BF16)
+            outs[number * blocks + i][...] = piece
 
     copies[0].wait()
-    expert_out = jnp.dot(act_ref[...], down[...], preferred_element_type=F32)
+    act = jnp.concatenate([a[...] for a in acts], axis=0)
+    expert_out = jnp.dot(act, down[...], preferred_element_type=F32)
     put((gate_col * expert_out).astype(BF16), 0)
     copies[1].wait()
     copies[2].wait()
-    grad = lax.dot_general(hid_ref[...], wide[...], NT, preferred_element_type=F32)
+    hidden_grads = jnp.concatenate([h[...] for h in hids], axis=0)
+    grad = lax.dot_general(hidden_grads, wide[...], NT, preferred_element_type=F32)
     put(grad.astype(BF16), 1)
 
 
-def rows_out(me, gate_arrays, act, hid, part, parts, wg, wu, wd, added, split):
-    blocks = len(gate_arrays)
+def rows_out(me, gate_arrays, acts, hids, part, wg, wu, wd, added):
+    blocks, groups = len(gate_arrays), len(acts)
     each = gate_arrays[0].shape[0]
-    rows = blocks * each
-    assert rows * parts == act.shape[0]
-    width, hidden_size = wg.shape
-    out = jax.ShapeDtypeStruct((rows // split, width), BF16)
+    width, hid = wg.shape
+    outs = (jax.ShapeDtypeStruct((each, width), BF16),) * (2 * blocks)
+    block = pl.BlockSpec((each, width), lambda i: (0, 0))
     gate_spec = pl.BlockSpec((each, LANES), lambda i: (0, width // LANES))
     return pl.pallas_call(
-        functools.partial(rows_kernel, blocks, len(added)),
-        out_shape=(out,) * (2 * split),
+        functools.partial(rows_kernel, blocks, groups, len(added)),
+        out_shape=outs,
         grid=(1,),
         in_specs=[SMEM]
         + [gate_spec] * blocks
-        + [pl.BlockSpec((rows, a.shape[1]), lambda i: (part, 0)) for a in (act, hid)]
+        + [pl.BlockSpec((a.shape[0] // 2, a.shape[1]), lambda i: (part, 0)) for a in (*acts, *hids)]
         + [ANY] * 3
-        + [pl.BlockSpec(a.shape, lambda i: (0, 0)) for a in added],
-        out_specs=(pl.BlockSpec(out.shape, lambda i: (0, 0)),) * (2 * split),
+        + [block] * len(added),
+        out_specs=(block,) * (2 * blocks),
         scratch_shapes=[
-            pltpu.VMEM((width, 2 * hidden_size), BF16),
-            pltpu.VMEM((hidden_size, width), BF16),
+            pltpu.VMEM((width, 2 * hid), BF16),
+            pltpu.VMEM((hid, width), BF16),
             pltpu.SemaphoreType.DMA((3,)),
         ],
         compiler_params=PARAMS,
-        cost_estimate=cost(6 * rows * width * hidden_size, (wg, wu, wd) + tuple(added) + (out,) * (2 * split)),
-    )(me, *gate_arrays, act, hid, wg, wu, wd, *added)
+        cost_estimate=cost(6 * blocks * each * width * hid, (wg, wu, wd) + outs),
+    )(me, *gate_arrays, *acts, *hids, wg, wu, wd, *added)
 
 
 def wide_grad_kernel(groups, first, count, order_ref, *refs):
@@ -268,15 +301,6 @@
     return (a.astype(F32) + b.astype(F32)).astype(BF16)
 
 
-def line_terms(parts, mid):
-    move = lambda a, pairs: lax.ppermute(a, "dp", pairs)
-    one = move(parts[0], [(0, 1), (1, 0), (2, 3), (3, 2)])
-    two = move(add(parts[1], jnp.where(mid, one, jnp.zeros_like(one))), [(0, 1), (1, 3), (3, 2), (2, 0)])
-    three = move(parts[2], [(0, 1), (3, 2)])
-    four = move(add(parts[2], two), [(1, 2), (2, 1)])
-    return (parts[3], one, two, three, four)
-
-
 LINE_ORDER = ((3, 2, 1, 0), (0, 3, 2, 1), (3, 0, 1, 2), (0, 1, 2, 3))
 
 
@@ -293,60 +317,85 @@
         return lax.ppermute(array, "expert", [(i, i ^ bit) for i in range(group)])
 
     cot_0 = cotangent
-    cot_y = flip(cot_0, FAR)
-    cot_x = flip(cot_0, NEAR)
-    lanes = jnp.arange(LANES, dtype=jnp.int32)[None, None, :]
-    spread = jnp.where(expert_ids[:, :, None] == lanes, gates.astype(F32)[:, :, None], 0.0)
-    tok_0 = jnp.concatenate([tokens, jnp.sum(spread, axis=1).astype(BF16)], axis=1)
-    tok_x = flip(tok_0, NEAR)
-    tok_y = flip(tok_0, FAR)
-    cot_d = flip(cot_y, NEAR)
-    tok_d = flip(tok_x, FAR)
+    tok_0 = packed(tokens, expert_ids, gates)
+    tok_x, cot_y = flip(tok_0, NEAR), flip(cot_0, FAR)
+    cot_x, tok_y = flip(cot_0, NEAR), flip(tok_0, FAR)
+    cot_d, tok_d = flip(cot_y, NEAR), flip(tok_x, FAR)
 
     toks_a, cots_a = [tok_0, tok_x, tok_y], [cot_0, cot_x, cot_y]
     toks_a += [flip(t, CORE) for t in toks_a]
     cots_a += [flip(c, CORE) for c in cots_a]
+    act_a, hid_a, act_t_a, hid_t_a, og_a = hidden(me, toks_a, cots_a, wg, wu, wd)
+    tok_d, cot_d = after((tok_d, cot_d), act_a)
     toks_b, cots_b = [tok_d, flip(tok_d, CORE)], [cot_d, flip(cot_d, CORE)]
-    act_a, hid_a, act_t_a, hid_t_a, og_a = hidden(me, toks_a, cots_a, wg, wu, wd)
     act_b, hid_b, act_t_b, hid_t_b, og_b = hidden(me, toks_b, cots_b, wg, wu, wd)
 
     line = shards == 4
     table = jnp.asarray(LINE_ORDER if line else ((0, 1, 2, 3),), jnp.int32)
     order = table[z if line else 0]
+    mid = (z == 1) | (z == 2)
+
+    def move(array, pairs):
+        return lax.ppermute(array, "dp", pairs) if line else array
+
+    def if_mid(array):
+        return jnp.where(mid, array, jnp.zeros_like(array))
+
+    one_pairs = [(0, 1), (1, 0), (2, 3), (3, 2)]
+    two_pairs = [(0, 1), (1, 3), (3, 2), (2, 0)]
+    up_pairs, down_pairs = [(0, 1), (1, 2)], [(3, 2), (2, 1)]
     toks = toks_a + toks_b
-    wide = wide_grads(order, toks, (hid_t_a, hid_t_b), width, 0, 1)
-    act_t_a, act_b = after((act_t_a, act_b), wide[0])
+    hid_t = (hid_t_a, hid_t_b)
+    wide_0 = wide_grads(order, toks, hid_t, width, 0, 1)
+    wide_one = move(wide_0[0], one_pairs)
+    act_t_a = after(act_t_a, wide_0)
     down = down_grads(order, (act_t_a, act_t_b), (og_a, og_b))
-    act_b, hid_t_a = after((act_b, hid_t_a), down[0])
-    out_s, grad_s = rows_out(me, toks_b[1:], act_b, hid_b, 1, 2, wg, wu, wd, (), 1)
-    hid_t_a = after(hid_t_a, out_s)
-    wide = wide + wide_grads(order, toks, (hid_t_a, hid_t_b), width, 1, 3)
-    added = after((flip(out_s, CORE), flip(grad_s, CORE)), wide[1])
-    out_d, grad_d = rows_out(me, toks_b[:1], act_b, hid_b, 0, 2, wg, wu, wd, added, 1)
-    act_a = after(act_a, out_d)
-    hid_size = wg.shape[1]
+    down_one = move(down[0], one_pairs)
+    hid_t_a = after(hid_t_a, down)
+    wide = wide_0 + wide_grads(order, toks, (hid_t_a, hid_t_b), width, 1, 3)
+    act_a = after(act_a, wide[1])
+    acts, hids = (act_a, act_b), (hid_a, hid_b)
+    sent = rows_out(me, toks_a[3:] + toks_b[1:], acts, hids, 1, wg, wu, wd, ())
     if line:
-        mid = (z == 1) | (z == 2)
-        wide_terms = line_terms(wide, mid)
-        down_terms = line_terms(down, mid)
-        grad_gate, grad_up = turn(mid.astype(jnp.int32).reshape(1), wide_terms)
-        own, one, two, three, four = (t.astype(F32) for t in down_terms)
-        grad_down = own + (three + four) + jnp.where(mid, 0.0, one + two)
+        wide_one = after(wide_one, sent)
+        wide_send = add(wide[1], if_mid(wide_one))
+        wide_two = move(wide_send, two_pairs)
+        down_one = after(down_one, wide_send)
+        down_send = add(down[1], if_mid(down_one))
+        down_two = move(down_send, two_pairs)
+        sent = after(sent, down_send)
+    sent = [flip(a, CORE) for a in sent]
+    kept = rows_out(me, toks_a[:3] + toks_b[:1], acts, hids, 0, wg, wu, wd, sent)
+    out_0, out_x, out_y, out_d, grad_0, grad_x, grad_y, grad_d = kept
+    out_dx, grad_dy = flip(out_d, NEAR), flip(grad_d, FAR)
+    out_xx, grad_yy = flip(out_x, NEAR), flip(grad_y, FAR)
+    hid_size = wd.shape[0]
+    if line:
+        wide_two = after(wide_two, kept)
+        wide_send = add(wide[2], if_mid(wide_two))
+        wide_up, wide_down = move(wide_send, up_pairs), move(wide_send, down_pairs)
+        down_two = after(down_two, wide_send)
+        down_send = add(down[2], if_mid(down_two))
+        down_up, down_down = move(down_send, up_pairs), move(down_send, down_pairs)
+        out_dx, grad_dy = after((out_dx, grad_dy), down_send)
+    out_yy = flip(add(out_y, out_dx), FAR)
+    grad_xx = flip(add(grad_x, grad_dy), NEAR)
+    mixed = (out_0.astype(F32) + out_xx.astype(F32) + out_yy.astype(F32)).astype(BF16)
+    grad_tokens = (grad_0.astype(F32) + grad_yy.astype(F32) + grad_xx.astype(F32)).astype(BF16)
+    if line:
+        wide_up, wide_down = after((wide_up, wide_down), (mixed, grad_tokens))
+        grad_gate, grad_up = turn(
+            mid.astype(jnp.int32).reshape(1), (wide[3], wide_one, wide_two, wide_up, wide_down)
+        )
+        own, one, two, up, low = (t.astype(F32) for t in (down[3], down_one, down_two, down_up, down_down))
+        grad_down = own + (up + low) + jnp.where(mid, 0.0, one + two)
     else:
         wide_all = jnp.concatenate(wide, axis=1).T
         grad_wide = lax.psum_scatter(wide_all, "dp", scatter_dimension=0, tiled=True).astype(F32)
         grad_gate, grad_up = grad_wide[:, :hid_size], grad_wide[:, hid_size:]
         grad_down = lax.psum_scatter(jnp.concatenate(down, axis=0), "dp", scatter_dimension=0, tiled=True).astype(F32)
 
-    out_s, grad_s = rows_out(me, toks_a[3:], act_a, hid_a, 1, 2, wg, wu, wd, (), 1)
-    out_0, out_x, out_y, grad_0, grad_x, grad_y = rows_out(
-        me, toks_a[:3], act_a, hid_a, 0, 2, wg, wu, wd, (flip(out_s, CORE), flip(grad_s, CORE)), 3
-    )
-    out_y = add(out_y, flip(out_d, NEAR))
-    grad_x = add(grad_x, flip(grad_d, FAR))
-    mixed = out_0.astype(F32) + flip(out_x, NEAR).astype(F32) + flip(out_y, FAR).astype(F32)
-    grad_tokens = grad_0.astype(F32) + flip(grad_y, FAR).astype(F32) + flip(grad_x, NEAR).astype(F32)
-    return (mixed.astype(BF16), grad_tokens.astype(BF16), grad_gate[None], grad_up[None], grad_down[None])
+    return (mixed, grad_tokens, grad_gate[None], grad_up[None], grad_down[None])
 
 
 def solution(mesh):

time: 184 us -> 159 us (0.86)
  waiting for transfers between devices: 68.7 us -> 57.4 us
  other arithmetic: 13.1 us -> 4.21 us
  Pallas kernels: 62.5 us -> 56.4 us
  local copies, waits for them, and re-layouts: 4.34 us -> 8.65 us
  starting transfers between devices: 33.8 us -> 30.8 us
    pallas_call x4 -> x3, Pallas kernels: 24.6 us -> 18 us  [the longest x2 15.8 us: rows_out(): pl.pallas_call(functools.partial(rows_kernel, blocks, groups, len(added))...]
    ppermute x8, waiting for transfers between devices: 33.9 us -> 27.9 us  [move(): return lax.ppermute(array, 'dp', pairs) if line else array]
    ppermute x24 -> x28, waiting for transfers between devices: 34.7 us -> 29.5 us  [flip(): return lax.ppermute(array, 'expert', [(i, i ^ bit) for i in range(group)])]
    unnamed x46 -> x68, local copies, waits for them, and re-layouts: 3.13 us -> 7.38 us
    convert_element_type x3 -> x2, other arithmetic: 5.21 us -> 2.06 us  [the longest x1 1.03 us: per_device(): (grad_0.astype(F32) + grad_yy.astype(F32) + grad_xx.astype(F32)).astype(B...]
    convert_element_type x6, other arithmetic: 3.67 us -> 0.96 us  [add(): return (a.astype(F32) + b.astype(F32)).astype(BF16)]
    ppermute x24 -> x28, starting transfers between devices: 15.1 us -> 14 us  [flip(): return lax.ppermute(array, 'expert', [(i, i ^ bit) for i in range(group)])]
  transfers between devices with their start and end apart: 32 -> 36, of which waited for: 7 -> 16; matrix products, arithmetic and copies ran while one was open for 5% -> 5% of each run, Pallas kernels for 22% -> 27%
where the time goes in v2:
time: 159 us
  waiting for transfers between devices  57.4 us (36%)
  Pallas kernels  56.4 us (35%)
  starting transfers between devices  30.8 us (19%)
  local copies, waits for them, and re-layouts  8.65 us (5%)
  other arithmetic  4.21 us (3%)
    ppermute x28, waiting for transfers between devices, flip(): return lax.ppermute(array, 'expert', [(i, i ^ bit) for i in range(group)])  29.5 us
    ppermute x8, waiting for transfers between devices, move(): return lax.ppermute(array, 'dp', pairs) if line else array  27.9 us
    ppermute x8, starting transfers between devices, move(): return lax.ppermute(array, 'dp', pairs) if line else array  16.8 us
    pallas_call x2, Pallas kernels, hidden(): pl.pallas_call(functools.partial(hidden_kernel, blocks), out_shape=outs,...  15.9 us
    pallas_call x2, Pallas kernels, rows_out(): pl.pallas_call(functools.partial(rows_kernel, blocks, groups, len(added))...  15.8 us
    ppermute x28, starting transfers between devices, flip(): return lax.ppermute(array, 'expert', [(i, i ^ bit) for i in range(group)])  14 us
    pallas_call x2, Pallas kernels, wide_grads(): pl.pallas_call(functools.partial(wide_grad_kernel, groups, first, count),...  11.8 us
    unnamed x68, local copies, waits for them, and re-layouts  7.38 us
  transfers between devices with their start and end apart: 36, of which 16 were waited for; matrix products, arithmetic and copies ran while one was open for 5% of the time, Pallas kernels for 27%

profile of v2, /device:TPU:10, one launch (start us, length us, event | category | flops | bytes accessed | tf_op | source)
XLA Modules:
  0.0 158.5 jit_solution(12266925483547563330)
XLA Ops:
  0.6 1.6 collective-permute-start.3
  2.8 1.4 copy.13.ids_ref
  4.2 1.4 copy.14.gates_ref
  5.6 2.1 %shard_map.119.refs_1_.refs_0_ = bf16[128,2176]{1,0:T(8,128)(2,1)} custom-call(bf16[128,2048]{1,0:T(8,128)(2,1)} %tok_ref.1, s32[128,4]{1,0:T(8,128)} %copy.13.ids_ref, bf16[128,4]{1,0:T(8,128)(2,1)} %copy.14.gates_ref), custom_call_target="tpu_custom_call" | custom-call | tf_op jit(solution)/shard_map/pallas_call | solution.py:45
  7.7 1.5 collective-permute-start
  9.7 6.1 %collective-permute-done.3.refs_9_ = bf16[128,2048]{1,0:T(8,128)(2,1)} collective-permute-done((bf16[128,2048]{1,0:T(8,128)(2,1)}, bf16[128,2048]{1,0:T(8,128)(2,1)}, u32[]{:S(2)}, u32[]{:S(2)}) %collective-permute-start.3) | collective-permute-done | bytes 524320 | tf_op jit(solution)/shard_map/ppermute | solution.py:317
  15.8 1.4 collective-permute-done.8.refs_8_
  17.3 10.5 %collective-permute-done.refs_2_.refs_1_ = bf16[128,2176]{1,0:T(8,128)(2,1)S(1)} collective-permute-done((bf16[128,2176]{1,0:T(8,128)(2,1)}, bf16[128,2176]{1,0:T(8,128)(2,1)S(1)}, u32[]{:S(2)}, u32[]{:S(2)}) %collective-permute-start) | collective-permute-done | bytes 557088 | tf_op jit(solution)/shard_map/ppermute | solution.py:317
  29.8 1.8 %collective-permute-done.10.refs_11_ = bf16[128,2048]{1,0:T(8,128)(2,1)} collective-permute-done((bf16[128,2048]{1,0:T(8,128)(2,1)}, bf16[128,2048]{1,0:T(8,128)(2,1)}, u32[]{:S(2)}, u32[]{:S(2)}) %collective-permute-start.10) | collective-permute-done | bytes 524320 | tf_op jit(solution)/shard_map/ppermute | solution.py:317
  32.6 10.5 %shard_map.120 = (bf16[768,384]{1,0:T(8,128)(2,1)}, bf16[768,768]{1,0:T(8,128)(2,1)}, bf16[384,768]{1,0:T(8,128)(2,1)}, bf16[768,768]{1,0:T(8,128)(2,1)}, bf16[768,2048]{1,0:T(8,128)(2,1)}) custom-call(s32[1]{0:T(128)} %bitcast.refs_0_, bf16[128,2176]{1,0:T(8,128)(2,1)} %shard_map.119.refs_1_.refs_0_, bf16[128,2176]{1,0:T(8,128)(2,1)} %copy-done.4, ...), custom_call_target="tpu_custom_call" | custom-call | flops 56623104 | bytes 279552 | tf_op jit(solution)/shard_map/pallas_call | solution.py:119
  48.3 5.5 %shard_map.121 = (bf16[256,384]{1,0:T(8,128)(2,1)}, bf16[256,768]{1,0:T(8,128)(2,1)}, bf16[384,256]{1,0:T(8,128)(2,1)}, bf16[768,256]{1,0:T(8,128)(2,1)}, bf16[256,2048]{1,0:T(8,128)(2,1)}) custom-call(s32[1]{0:T(128)} %bitcast.refs_0_, bf16[128,2176]{1,0:T(8,128)(2,1)} %copy-done.6, bf16[128,2176]{1,0:T(8,128)(2,1)} %copy-done.3, ...), custom_call_target="tpu_custom_call" | custom-call | flops 18874368 | bytes 142336 | tf_op jit(solution)/shard_map/pallas_call | solution.py:119
  53.7 4.3 %shard_map.122 = bf16[768,512]{1,0:T(8,128)(2,1)} custom-call(s32[4]{0:T(128)} %dynamic-slice_bitcast_fusion.order_ref, bf16[128,2176]{1,0:T(8,128)(2,1)} %shard_map.119.refs_1_.refs_0_, bf16[128,2176]{1,0:T(8,128)(2,1)} %copy-done.4, bf16[128,2176]{1,0:T(8,128)(2,1)} %copy-done.5, bf16[128,2176]{1,0:T(8,128)(2,1)} %copy-done, bf16[128,2176]{1,0:T(8,128)(2,1)} %copy-done.1, ...), custom_call_target="tpu_custom_call" | custom-call | flops 12582912 | bytes 36864 | tf_op jit(solution)/shard_map/pallas_call | solution.py:223
  58.5 6.3 %shard_map.123 = (bf16[96,2048]{1,0:T(8,128)(2,1)}, bf16[96,2048]{1,0:T(8,128)(2,1)}, bf16[96,2048]{1,0:T(8,128)(2,1)}, bf16[96,2048]{1,0:T(8,128)(2,1)}) custom-call(s32[4]{0:T(128)} %dynamic-slice_bitcast_fusion.order_ref, bf16[384,768]{1,0:T(8,128)(2,1)} %get-tuple-element.67.refs_0_, bf16[384,256]{1,0:T(8,128)(2,1)} %get-tuple-element.68.refs_1_, ...), custom_call_target="tpu_custom_call" | custom-call | flops 25165824 | bytes 77824 | tf_op jit(solution)/shard_map/pallas_call | solution.py:257
  64.8 1.6 %collective-permute-start.14 = (bf16[96,2048]{1,0:T(8,128)(2,1)}, bf16[96,2048]{1,0:T(8,128)(2,1)S(1)}, u32[]{:S(2)}, u32[]{:S(2)}) collective-permute-start(bf16[96,2048]{1,0:T(8,128)(2,1)} %get-tuple-element.71), channel_id=1, source_target_pairs={{0,8},{8,0},{16,24},{24,16},{1,9},{9,1},{17,25},{25,17},{2,10},{10... | collective-permute-start | bytes 1179656 | tf_op jit(solution)/shard_map/ppermute | solution.py:339
  66.4 7.5 %shard_map.124 = (bf16[768,512]{1,0:T(8,128)(2,1)}, bf16[768,512]{1,0:T(8,128)(2,1)}, bf16[768,512]{1,0:T(8,128)(2,1)}) custom-call(s32[4]{0:T(128)} %dynamic-slice_bitcast_fusion.order_ref, bf16[128,2176]{1,0:T(8,128)(2,1)} %shard_map.119.refs_1_.refs_0_, bf16[128,2176]{1,0:T(8,128)(2,1)} %copy-done.4, bf16[128,2176]{1,0:T(8,128)(2,1)} %copy-done.5, ...), custom_call_target="tpu_custom_call" | custom-call | flops 37748736 | bytes 61440 | tf_op jit(solution)/shard_map/pallas_call | solution.py:223
  73.9 7.2 %shard_map.125 = (bf16[128,2048]{1,0:T(8,128)(2,1)}, bf16[128,2048]{1,0:T(8,128)(2,1)}, bf16[128,2048]{1,0:T(8,128)(2,1)}, bf16[128,2048]{1,0:T(8,128)(2,1)}, bf...) custom-call(s32[1]{0:T(128)} %bitcast.refs_0_, ...), custom_call_target="tpu_custom_call" | custom-call | flops 37748736 | bytes 139264 | tf_op jit(solution)/shard_map/pallas_call | solution.py:180
  81.5 4.8 %collective-permute-done.14 = bf16[96,2048]{1,0:T(8,128)(2,1)S(1)} collective-permute-done((bf16[96,2048]{1,0:T(8,128)(2,1)}, bf16[96,2048]{1,0:T(8,128)(2,1)S(1)}, u32[]{:S(2)}, u32[]{:S(2)}) %collective-permute-start.14) | collective-permute-done | bytes 393248 | tf_op jit(solution)/shard_map/ppermute | solution.py:339
  87.5 2.6 %collective-permute-start.28 = (bf16[768,512]{1,0:T(8,128)(2,1)S(1)}, bf16[768,512]{1,0:T(8,128)(2,1)S(1)}, u32[]{:S(2)}, u32[]{:S(2)}) collective-permute-start(bf16[768,512]{1,0:T(8,128)(2,1)S(1)} %add_convert_fusion.1), channel_id=1, source_target_pairs={{0,8},{8,24},{24,16},{16,0},{1,9},{9,25},{25,17},{17,1},{2,10},{10... | collective-permute-start | bytes 2359304 | tf_op jit(solution)/shard_map/ppermute | solution.py:339
  92.9 2.7 %collective-permute-start.27 = (bf16[96,2048]{1,0:T(8,128)(2,1)S(1)}, bf16[96,2048]{1,0:T(8,128)(2,1)S(1)}, u32[]{:S(2)}, u32[]{:S(2)}) collective-permute-start(bf16[96,2048]{1,0:T(8,128)(2,1)S(1)} %add_convert_fusion.7), channel_id=1, source_target_pairs={{0,8},{8,24},{24,16},{16,0},{1,9},{9,25},{25,17},{17,1},{2,10},{10... | collective-permute-start | bytes 1179656 | tf_op jit(solution)/shard_map/ppermute | solution.py:339
  95.6 8.7 %shard_map.126 = (bf16[128,2048]{1,0:T(8,128)(2,1)}, bf16[128,2048]{1,0:T(8,128)(2,1)}, bf16[128,2048]{1,0:T(8,128)(2,1)}, bf16[128,2048]{1,0:T(8,128)(2,1)}, bf...) custom-call(s32[1]{0:T(128)} %bitcast.refs_0_, ...), custom_call_target="tpu_custom_call" | custom-call | flops 37748736 | bytes 139264 | tf_op jit(solution)/shard_map/pallas_call | solution.py:180
  104.8 1.4 collective-permute-start.26
  108.8 6.8 %collective-permute-done.27 = bf16[96,2048]{1,0:T(8,128)(2,1)S(1)} collective-permute-done((bf16[96,2048]{1,0:T(8,128)(2,1)S(1)}, bf16[96,2048]{1,0:T(8,128)(2,1)S(1)}, u32[]{:S(2)}, u32[]{:S(2)}) %collective-permute-start.27) | collective-permute-done | bytes 393248 | tf_op jit(solution)/shard_map/ppermute | solution.py:339
  115.7 3.5 %collective-permute-start.34 = (bf16[96,2048]{1,0:T(8,128)(2,1)S(1)}, bf16[96,2048]{1,0:T(8,128)(2,1)S(1)}, u32[]{:S(2)}, u32[]{:S(2)}) collective-permute-start(bf16[96,2048]{1,0:T(8,128)(2,1)S(1)} %add_convert_fusion.6), channel_id=1, source_target_pairs={{0,8},{8,16},{1,9},{9,17},{2,10},{10,18},{3,11},{11,19},{4,12},{12... | collective-permute-start | bytes 1179656 | tf_op jit(solution)/shard_map/ppermute | solution.py:339
  121.7 6.3 %collective-permute-done.34 = bf16[96,2048]{1,0:T(8,128)(2,1)S(1)} collective-permute-done((bf16[96,2048]{1,0:T(8,128)(2,1)S(1)}, bf16[96,2048]{1,0:T(8,128)(2,1)S(1)}, u32[]{:S(2)}, u32[]{:S(2)}) %collective-permute-start.34) | collective-permute-done | bytes 393248 | tf_op jit(solution)/shard_map/ppermute | solution.py:339
  128.0 3.4 %collective-permute-start.32 = (bf16[768,512]{1,0:T(8,128)(2,1)S(1)}, bf16[768,512]{1,0:T(8,128)(2,1)S(1)}, u32[]{:S(2)}, u32[]{:S(2)}) collective-permute-start(bf16[768,512]{1,0:T(8,128)(2,1)S(1)} %add_convert_fusion), channel_id=1, source_target_pairs={{0,8},{8,16},{1,9},{9,17},{2,10},{10,18},{3,11},{11,19},{4,12},{12... | collective-permute-start | bytes 2359304 | tf_op jit(solution)/shard_map/ppermute | solution.py:339
  131.4 1.4 collective-permute-start.29
  134.0 1.4 collective-permute-start.33
  135.5 5.2 %collective-permute-done.31 = bf16[128,2048]{1,0:T(8,128)(2,1)S(1)} collective-permute-done((bf16[128,2048]{1,0:T(8,128)(2,1)S(1)}, bf16[128,2048]{1,0:T(8,128)(2,1)S(1)}, u32[]{:S(2)}, u32[]{:S(2)}) %collective-permute-start.31) | collective-permute-done | bytes 524320 | tf_op jit(solution)/shard_map/ppermute | solution.py:317
  141.7 1.6 %collective-permute-done.29 = bf16[128,2048]{1,0:T(8,128)(2,1)S(1)} collective-permute-done((bf16[128,2048]{1,0:T(8,128)(2,1)S(1)}, bf16[128,2048]{1,0:T(8,128)(2,1)S(1)}, u32[]{:S(2)}, u32[]{:S(2)}) %collective-permute-start.29) | collective-permute-done | bytes 524320 | tf_op jit(solution)/shard_map/ppermute | solution.py:317
  144.4 3.3 %collective-permute-done.32.a3 = bf16[768,512]{1,0:T(8,128)(2,1)S(1)} collective-permute-done((bf16[768,512]{1,0:T(8,128)(2,1)S(1)}, bf16[768,512]{1,0:T(8,128)(2,1)S(1)}, u32[]{:S(2)}, u32[]{:S(2)}) %collective-permute-start.32) | collective-permute-done | bytes 786464 | tf_op jit(solution)/shard_map/ppermute | solution.py:339
  147.7 5.6 %collective-permute-done.33.a4 = bf16[768,512]{1,0:T(8,128)(2,1)S(1)} collective-permute-done((bf16[768,512]{1,0:T(8,128)(2,1)S(1)}, bf16[768,512]{1,0:T(8,128)(2,1)S(1)}, u32[]{:S(2)}, u32[]{:S(2)}) %collective-permute-start.33) | collective-permute-done | bytes 786464 | tf_op jit(solution)/shard_map/ppermute | solution.py:339
  154.1 4.4 %shard_map.127 = (f32[512,384]{1,0:T(8,128)}, f32[512,384]{1,0:T(8,128)}) custom-call(s32[1]{0:T(128)} %bitcast.5.mid_ref, bf16[768,512]{1,0:T(8,128)(2,1)} %get-tuple-element.112.own, bf16[768,512]{1,0:T(8,128)(2,1)} %copy-done.7, bf16[768,512]{1,0:T(8,128)(2,1)} %copy-done.8, bf16[768,512]{1,0:T(8,128)(2,1)} %copy-done.11, bf16[768,512]{1,0:T(8,128)(2,1)} %copy-done.12), custom_call_target="tpu_custom_call" | custom-call | flops 30720 | bytes 86016 | tf_op jit(solution)/shard_map/pallas_call | solution.py:285
  (127 shorter events, 23.8 us)
Async XLA Ops:
  0.6 15.2 %collective-permute-start.3 = (bf16[128,2048]{1,0:T(8,128)(2,1)}, bf16[128,2048]{1,0:T(8,128)(2,1)}, u32[]{:S(2)}, u32[]{:S(2)}) collective-permute-start(bf16[128,2048]{1,0:T(8,128)(2,1)} %refs_7_.1), channel_id=1, source_target_pairs={{0,4},{1,5},{2,6},{3,7},{4,0},{5,1},{6,2},{7,3},{8,12},{9,13},{10,... | collective-permute-start | bytes 1572872 | tf_op jit(solution)/shard_map/ppermute | solution.py:317
  2.2 15.1 %collective-permute-start.8 = (bf16[128,2048]{1,0:T(8,128)(2,1)}, bf16[128,2048]{1,0:T(8,128)(2,1)S(1)}, u32[]{:S(2)}, u32[]{:S(2)}) collective-permute-start(bf16[128,2048]{1,0:T(8,128)(2,1)} %refs_7_.1), channel_id=1, source_target_pairs={{0,2},{1,3},{2,0},{3,1},{4,6},{5,7},{6,4},{7,5},{8,10},{9,11},{10,... | collective-permute-start | bytes 1572872 | tf_op jit(solution)/shard_map/ppermute | solution.py:317
  7.7 20.1 %collective-permute-start = (bf16[128,2176]{1,0:T(8,128)(2,1)}, bf16[128,2176]{1,0:T(8,128)(2,1)S(1)}, u32[]{:S(2)}, u32[]{:S(2)}) collective-permute-start(bf16[128,2176]{1,0:T(8,128)(2,1)} %shard_map.119.refs_1_.refs_0_), channel_id=1, source_target_pairs={{0,2},{1,3},{2,0},{3,1},{4,6},{5,7},{6,4},{7,5},{8,10},{9,11},{10,... | collective-permute-start | bytes 1671176 | tf_op jit(solution)/shard_map/ppermute | solution.py:317
  9.2 18.6 %collective-permute-start.1 = (bf16[128,2176]{1,0:T(8,128)(2,1)}, bf16[128,2176]{1,0:T(8,128)(2,1)S(1)}, u32[]{:S(2)}, u32[]{:S(2)}) collective-permute-start(bf16[128,2176]{1,0:T(8,128)(2,1)} %shard_map.119.refs_1_.refs_0_), channel_id=1, source_target_pairs={{0,4},{1,5},{2,6},{3,7},{4,0},{5,1},{6,2},{7,3},{8,12},{9,13},{10,... | collective-permute-start | bytes 1671176 | tf_op jit(solution)/shard_map/ppermute | solution.py:317
  9.7 19.2 %collective-permute-start.5 = (bf16[128,2176]{1,0:T(8,128)(2,1)}, bf16[128,2176]{1,0:T(8,128)(2,1)S(1)}, u32[]{:S(2)}, u32[]{:S(2)}) collective-permute-start(bf16[128,2176]{1,0:T(8,128)(2,1)} %shard_map.119.refs_1_.refs_0_), channel_id=1, source_target_pairs={{0,1},{1,0},{2,3},{3,2},{4,5},{5,4},{6,7},{7,6},{8,9},{9,8},{10,11... | collective-permute-start | bytes 1671176 | tf_op jit(solution)/shard_map/ppermute | solution.py:317
  15.8 12.4 %collective-permute-start.9 = (bf16[128,2048]{1,0:T(8,128)(2,1)}, bf16[128,2048]{1,0:T(8,128)(2,1)S(1)}, u32[]{:S(2)}, u32[]{:S(2)}) collective-permute-start(bf16[128,2048]{1,0:T(8,128)(2,1)} %refs_7_.1), channel_id=1, source_target_pairs={{0,1},{1,0},{2,3},{3,2},{4,5},{5,4},{6,7},{7,6},{8,9},{9,8},{10,11... | collective-permute-start | bytes 1572872 | tf_op jit(solution)/shard_map/ppermute | solution.py:317
  17.3 12.0 %collective-permute-start.11 = (bf16[128,2048]{1,0:T(8,128)(2,1)}, bf16[128,2048]{1,0:T(8,128)(2,1)}, u32[]{:S(2)}, u32[]{:S(2)}) collective-permute-start(bf16[128,2048]{1,0:T(8,128)(2,1)} %collective-permute-done.3.refs_9_), channel_id=1, source_target_pairs={{0,1},{1,0},{2,3},{3,2},{4,5},{5,4},{6,7},{7,6},{8,9},{9,8},{10,11... | collective-permute-start | bytes 1572872 | tf_op jit(solution)/shard_map/ppermute | solution.py:317
  27.8 3.8 %collective-permute-start.6 = (bf16[128,2176]{1,0:T(8,128)(2,1)S(1)}, bf16[128,2176]{1,0:T(8,128)(2,1)S(1)}, u32[]{:S(2)}, u32[]{:S(2)}) collective-permute-start(bf16[128,2176]{1,0:T(8,128)(2,1)S(1)} %collective-permute-done.refs_2_.refs_1_), channel_id=1, source_target_pairs={{0,1},{1,0},{2,3},{3,2},{4,5},{5,4},{6,7},{7,6},{8,9},{9,8},{10,11... | collective-permute-start | bytes 1671176 | tf_op jit(solution)/shard_map/ppermute | solution.py:317
  27.8 3.8 %collective-permute-start.7 = (bf16[128,2176]{1,0:T(8,128)(2,1)S(1)}, bf16[128,2176]{1,0:T(8,128)(2,1)S(1)}, u32[]{:S(2)}, u32[]{:S(2)}) collective-permute-start(bf16[128,2176]{1,0:T(8,128)(2,1)S(1)} %collective-permute-done.1.refs_3_.refs_2_), channel_id=1, source_target_pairs={{0,1},{1,0},{2,3},{3,2},{4,5},{5,4},{6,7},{7,6},{8,9},{9,8},{10,11... | collective-permute-start | bytes 1671176 | tf_op jit(solution)/shard_map/ppermute | solution.py:317
  28.3 15.5 %collective-permute-start.2 = (bf16[128,2176]{1,0:T(8,128)(2,1)S(1)}, bf16[128,2176]{1,0:T(8,128)(2,1)S(1)}, u32[]{:S(2)}, u32[]{:S(2)}) collective-permute-start(bf16[128,2176]{1,0:T(8,128)(2,1)S(1)} %collective-permute-done.refs_2_.refs_1_), channel_id=1, source_target_pairs={{0,4},{1,5},{2,6},{3,7},{4,0},{5,1},{6,2},{7,3},{8,12},{9,13},{10,... | collective-permute-start | bytes 1671176 | tf_op jit(solution)/shard_map/ppermute | solution.py:317
  29.3 14.5 %collective-permute-start.4 = (bf16[128,2048]{1,0:T(8,128)(2,1)}, bf16[128,2048]{1,0:T(8,128)(2,1)}, u32[]{:S(2)}, u32[]{:S(2)}) collective-permute-start(bf16[128,2048]{1,0:T(8,128)(2,1)} %collective-permute-done.3.refs_9_), channel_id=1, source_target_pairs={{0,2},{1,3},{2,0},{3,1},{4,6},{5,7},{6,4},{7,5},{8,10},{9,11},{10,... | collective-permute-start | bytes 1572872 | tf_op jit(solution)/shard_map/ppermute | solution.py:317
  58.1 23.1 %collective-permute-start.15 = (bf16[768,512]{1,0:T(8,128)(2,1)}, bf16[768,512]{1,0:T(8,128)(2,1)S(1)}, u32[]{:S(2)}, u32[]{:S(2)}) collective-permute-start(bf16[768,512]{1,0:T(8,128)(2,1)} %shard_map.122), channel_id=1, source_target_pairs={{0,8},{8,0},{16,24},{24,16},{1,9},{9,1},{17,25},{25,17},{2,10},{10... | collective-permute-start | bytes 2359304 | tf_op jit(solution)/shard_map/ppermute | solution.py:339
  64.8 21.4 %collective-permute-start.14 = (bf16[96,2048]{1,0:T(8,128)(2,1)}, bf16[96,2048]{1,0:T(8,128)(2,1)S(1)}, u32[]{:S(2)}, u32[]{:S(2)}) collective-permute-start(bf16[96,2048]{1,0:T(8,128)(2,1)} %get-tuple-element.71), channel_id=1, source_target_pairs={{0,8},{8,0},{16,24},{24,16},{1,9},{9,1},{17,25},{25,17},{2,10},{10... | collective-permute-start | bytes 1179656 | tf_op jit(solution)/shard_map/ppermute | solution.py:339
  86.4 3.7 %collective-permute-start.16 = (bf16[128,2048]{1,0:T(8,128)(2,1)S(1)}, bf16[128,2048]{1,0:T(8,128)(2,1)S(1)}, u32[]{:S(2)}, u32[]{:S(2)}) collective-permute-start(bf16[128,2048]{1,0:T(8,128)(2,1)S(1)} %copy-done.32), channel_id=1, source_target_pairs={{0,1},{1,0},{2,3},{3,2},{4,5},{5,4},{6,7},{7,6},{8,9},{9,8},{10,11... | collective-permute-start | bytes 1572872 | tf_op jit(solution)/shard_map/ppermute | solution.py:317
  86.5 3.7 %collective-permute-start.17 = (bf16[128,2048]{1,0:T(8,128)(2,1)S(1)}, bf16[128,2048]{1,0:T(8,128)(2,1)S(1)}, u32[]{:S(2)}, u32[]{:S(2)}) collective-permute-start(bf16[128,2048]{1,0:T(8,128)(2,1)S(1)} %copy-done.31), channel_id=1, source_target_pairs={{0,1},{1,0},{2,3},{3,2},{4,5},{5,4},{6,7},{7,6},{8,9},{9,8},{10,11... | collective-permute-start | bytes 1572872 | tf_op jit(solution)/shard_map/ppermute | solution.py:317
  87.0 3.7 %collective-permute-start.18 = (bf16[128,2048]{1,0:T(8,128)(2,1)S(1)}, bf16[128,2048]{1,0:T(8,128)(2,1)S(1)}, u32[]{:S(2)}, u32[]{:S(2)}) collective-permute-start(bf16[128,2048]{1,0:T(8,128)(2,1)S(1)} %copy-done.30), channel_id=1, source_target_pairs={{0,1},{1,0},{2,3},{3,2},{4,5},{5,4},{6,7},{7,6},{8,9},{9,8},{10,11... | collective-permute-start | bytes 1572872 | tf_op jit(solution)/shard_map/ppermute | solution.py:317
  87.1 3.7 %collective-permute-start.19 = (bf16[128,2048]{1,0:T(8,128)(2,1)S(1)}, bf16[128,2048]{1,0:T(8,128)(2,1)S(1)}, u32[]{:S(2)}, u32[]{:S(2)}) collective-permute-start(bf16[128,2048]{1,0:T(8,128)(2,1)S(1)} %copy-done.29), channel_id=1, source_target_pairs={{0,1},{1,0},{2,3},{3,2},{4,5},{5,4},{6,7},{7,6},{8,9},{9,8},{10,11... | collective-permute-start | bytes 1572872 | tf_op jit(solution)/shard_map/ppermute | solution.py:317
  87.5 20.5 %collective-permute-start.28 = (bf16[768,512]{1,0:T(8,128)(2,1)S(1)}, bf16[768,512]{1,0:T(8,128)(2,1)S(1)}, u32[]{:S(2)}, u32[]{:S(2)}) collective-permute-start(bf16[768,512]{1,0:T(8,128)(2,1)S(1)} %add_convert_fusion.1), channel_id=1, source_target_pairs={{0,8},{8,24},{24,16},{16,0},{1,9},{9,25},{25,17},{17,1},{2,10},{10... | collective-permute-start | bytes 2359304 | tf_op jit(solution)/shard_map/ppermute | solution.py:339
  90.2 5.3 %collective-permute-start.21 = (bf16[128,2048]{1,0:T(8,128)(2,1)}, bf16[128,2048]{1,0:T(8,128)(2,1)}, u32[]{:S(2)}, u32[]{:S(2)}) collective-permute-start(bf16[128,2048]{1,0:T(8,128)(2,1)} %get-tuple-element.96), channel_id=1, source_target_pairs={{0,1},{1,0},{2,3},{3,2},{4,5},{5,4},{6,7},{7,6},{8,9},{9,8},{10,11... | collective-permute-start | bytes 1572872 | tf_op jit(solution)/shard_map/ppermute | solution.py:317
  90.7 4.9 %collective-permute-start.22 = (bf16[128,2048]{1,0:T(8,128)(2,1)}, bf16[128,2048]{1,0:T(8,128)(2,1)}, u32[]{:S(2)}, u32[]{:S(2)}) collective-permute-start(bf16[128,2048]{1,0:T(8,128)(2,1)} %get-tuple-element.97), channel_id=1, source_target_pairs={{0,1},{1,0},{2,3},{3,2},{4,5},{5,4},{6,7},{7,6},{8,9},{9,8},{10,11... | collective-permute-start | bytes 1572872 | tf_op jit(solution)/shard_map/ppermute | solution.py:317
  90.8 4.8 %collective-permute-start.23 = (bf16[128,2048]{1,0:T(8,128)(2,1)}, bf16[128,2048]{1,0:T(8,128)(2,1)}, u32[]{:S(2)}, u32[]{:S(2)}) collective-permute-start(bf16[128,2048]{1,0:T(8,128)(2,1)} %get-tuple-element.98), channel_id=1, source_target_pairs={{0,1},{1,0},{2,3},{3,2},{4,5},{5,4},{6,7},{7,6},{8,9},{9,8},{10,11... | collective-permute-start | bytes 1572872 | tf_op jit(solution)/shard_map/ppermute | solution.py:317
  92.9 22.7 %collective-permute-start.27 = (bf16[96,2048]{1,0:T(8,128)(2,1)S(1)}, bf16[96,2048]{1,0:T(8,128)(2,1)S(1)}, u32[]{:S(2)}, u32[]{:S(2)}) collective-permute-start(bf16[96,2048]{1,0:T(8,128)(2,1)S(1)} %add_convert_fusion.7), channel_id=1, source_target_pairs={{0,8},{8,24},{24,16},{16,0},{1,9},{9,25},{25,17},{17,1},{2,10},{10... | collective-permute-start | bytes 1179656 | tf_op jit(solution)/shard_map/ppermute | solution.py:339
  104.2 15.1 %collective-permute-start.25 = (bf16[128,2048]{1,0:T(8,128)(2,1)}, bf16[128,2048]{1,0:T(8,128)(2,1)S(1)}, u32[]{:S(2)}, u32[]{:S(2)}) collective-permute-start(bf16[128,2048]{1,0:T(8,128)(2,1)} %get-tuple-element.102), channel_id=1, source_target_pairs={{0,2},{1,3},{2,0},{3,1},{4,6},{5,7},{6,4},{7,5},{8,10},{9,11},{10,... | collective-permute-start | bytes 1572872 | tf_op jit(solution)/shard_map/ppermute | solution.py:317
  104.8 15.8 %collective-permute-start.26 = (bf16[128,2048]{1,0:T(8,128)(2,1)}, bf16[128,2048]{1,0:T(8,128)(2,1)S(1)}, u32[]{:S(2)}, u32[]{:S(2)}) collective-permute-start(bf16[128,2048]{1,0:T(8,128)(2,1)} %get-tuple-element.103), channel_id=1, source_target_pairs={{0,4},{1,5},{2,6},{3,7},{4,0},{5,1},{6,2},{7,3},{8,12},{9,13},{10,... | collective-permute-start | bytes 1572872 | tf_op jit(solution)/shard_map/ppermute | solution.py:317
  106.2 27.8 %collective-permute-start.30 = (bf16[128,2048]{1,0:T(8,128)(2,1)}, bf16[128,2048]{1,0:T(8,128)(2,1)S(1)}, u32[]{:S(2)}, u32[]{:S(2)}) collective-permute-start(bf16[128,2048]{1,0:T(8,128)(2,1)} %get-tuple-element.107), channel_id=1, source_target_pairs={{0,4},{1,5},{2,6},{3,7},{4,0},{5,1},{6,2},{7,3},{8,12},{9,13},{10,... | collective-permute-start | bytes 1572872 | tf_op jit(solution)/shard_map/ppermute | solution.py:317
  108.0 33.7 %collective-permute-start.24 = (bf16[128,2048]{1,0:T(8,128)(2,1)}, bf16[128,2048]{1,0:T(8,128)(2,1)S(1)}, u32[]{:S(2)}, u32[]{:S(2)}) collective-permute-start(bf16[128,2048]{1,0:T(8,128)(2,1)} %get-tuple-element.100), channel_id=1, source_target_pairs={{0,2},{1,3},{2,0},{3,1},{4,6},{5,7},{6,4},{7,5},{8,10},{9,11},{10,... | collective-permute-start | bytes 1572872 | tf_op jit(solution)/shard_map/ppermute | solution.py:317
  115.7 12.3 %collective-permute-start.34 = (bf16[96,2048]{1,0:T(8,128)(2,1)S(1)}, bf16[96,2048]{1,0:T(8,128)(2,1)S(1)}, u32[]{:S(2)}, u32[]{:S(2)}) collective-permute-start(bf16[96,2048]{1,0:T(8,128)(2,1)S(1)} %add_convert_fusion.6), channel_id=1, source_target_pairs={{0,8},{8,16},{1,9},{9,17},{2,10},{10,18},{3,11},{11,19},{4,12},{12... | collective-permute-start | bytes 1179656 | tf_op jit(solution)/shard_map/ppermute | solution.py:339
  119.3 12.1 %collective-permute-start.35 = (bf16[96,2048]{1,0:T(8,128)(2,1)S(1)}, bf16[96,2048]{1,0:T(8,128)(2,1)S(1)}, u32[]{:S(2)}, u32[]{:S(2)}) collective-permute-start(bf16[96,2048]{1,0:T(8,128)(2,1)S(1)} %add_convert_fusion.6), channel_id=1, source_target_pairs={{24,16},{16,8},{25,17},{17,9},{26,18},{18,10},{27,19},{19,11},{28,... | collective-permute-start | bytes 1179656 | tf_op jit(solution)/shard_map/ppermute | solution.py:339
  120.8 19.9 %collective-permute-start.31 = (bf16[128,2048]{1,0:T(8,128)(2,1)S(1)}, bf16[128,2048]{1,0:T(8,128)(2,1)S(1)}, u32[]{:S(2)}, u32[]{:S(2)}) collective-permute-start(bf16[128,2048]{1,0:T(8,128)(2,1)S(1)} %add_convert_fusion.3), channel_id=1, source_target_pairs={{0,2},{1,3},{2,0},{3,1},{4,6},{5,7},{6,4},{7,5},{8,10},{9,11},{10,... | collective-permute-start | bytes 1572872 | tf_op jit(solution)/shard_map/ppermute | solution.py:317
  128.0 19.6 %collective-permute-start.32 = (bf16[768,512]{1,0:T(8,128)(2,1)S(1)}, bf16[768,512]{1,0:T(8,128)(2,1)S(1)}, u32[]{:S(2)}, u32[]{:S(2)}) collective-permute-start(bf16[768,512]{1,0:T(8,128)(2,1)S(1)} %add_convert_fusion), channel_id=1, source_target_pairs={{0,8},{8,16},{1,9},{9,17},{2,10},{10,18},{3,11},{11,19},{4,12},{12... | collective-permute-start | bytes 2359304 | tf_op jit(solution)/shard_map/ppermute | solution.py:339
  131.4 11.9 %collective-permute-start.29 = (bf16[128,2048]{1,0:T(8,128)(2,1)S(1)}, bf16[128,2048]{1,0:T(8,128)(2,1)S(1)}, u32[]{:S(2)}, u32[]{:S(2)}) collective-permute-start(bf16[128,2048]{1,0:T(8,128)(2,1)S(1)} %add_convert_fusion.5), channel_id=1, source_target_pairs={{0,4},{1,5},{2,6},{3,7},{4,0},{5,1},{6,2},{7,3},{8,12},{9,13},{10,... | collective-permute-start | bytes 1572872 | tf_op jit(solution)/shard_map/ppermute | solution.py:317
  134.0 19.2 %collective-permute-start.33 = (bf16[768,512]{1,0:T(8,128)(2,1)S(1)}, bf16[768,512]{1,0:T(8,128)(2,1)S(1)}, u32[]{:S(2)}, u32[]{:S(2)}) collective-permute-start(bf16[768,512]{1,0:T(8,128)(2,1)S(1)} %add_convert_fusion), channel_id=1, source_target_pairs={{24,16},{16,8},{25,17},{17,9},{26,18},{18,10},{27,19},{19,11},{28,... | collective-permute-start | bytes 2359304 | tf_op jit(solution)/shard_map/ppermute | solution.py:339
  (37 other events, 202.8 us)
